TPU v7x, 32 devices: a whole 2x2x4 slice. The times are simulated.
32 devices in a mesh: graph: 16 (over z, y, x), head: 2 (over core).
Axes of the slice: x: 2, y: 2, z: 4, core: 2. Of those that a mesh axis runs over, the one named last changes fastest.
Arguments:
- node_input: bfloat16 [32768, 512], P('graph', 'head'), may hold values from -6 to 6
- cotangent: bfloat16 [32768, 512], P('graph', 'head'), may hold values from -6 to 6
- norm_gain: bfloat16 [512], P('head'), may hold values from 0.5 to 1.5
- norm_bias: bfloat16 [512], P('head'), may hold values from -3 to 3
- query_weight: bfloat16 [512, 512], P(None, 'head'), may hold values from -0.25 to 0.25
- key_weight: bfloat16 [512, 512], P(None, 'head'), may hold values from -0.25 to 0.25
- value_weight: bfloat16 [512, 512], P(None, 'head'), may hold values from -0.25 to 0.25
- gate_weight: bfloat16 [512, 512], P(None, 'head'), may hold values from -0.25 to 0.25
- out_weight: bfloat16 [512, 512], P(None, 'head'), may hold values from -0.5 to 0.5
- adjacent_vertices: int32 [32768, 16], P('graph'), may hold values from 0 to 127, as said below
- active_vertex_tally: int32 [256], P('graph'), may hold values from 32 to 128, as said below
- training_period: int32 [256], P('graph'), may hold values 0 or 1
Outputs:
- layer_output: bfloat16 [32768, 512], P('graph', 'head')
- input_grad: bfloat16 [32768, 512], P('graph', 'head')
- gain_grad: float32 [512], P('head')
- bias_grad: float32 [512], P('head')
- query_grad: float32 [512, 512], P(None, 'head')
- key_grad: float32 [512, 512], P(None, 'head')
- value_grad: float32 [512, 512], P(None, 'head')
- gate_grad: float32 [512, 512], P(None, 'head')
- out_grad: float32 [512, 512], P(None, 'head')
Inputs may be any that keep to these rules, and one draw needn't show every extreme that they name: `active_vertex_tally`: each index of graph holds one subgraph of 128 live nodes. `adjacent_vertices`: every entry names a live node of the row's own subgraph (below its node count).
All inputs are finite; a program needn't handle non-finite values. No bound on the sum of `training_period` on one device may be relied on, other than what follows from the above.
Results may differ from a plain program's by a relative error of at most 0.0025.
The roundings to bfloat16 on the way count: a program that leaves them out, or rounds other values in their place, can miss the bound.
Values may be sent and summed in bfloat16 or wider, within the bound.
A program may use at most 128 MiB of HBM per device.

v0:
```python
import jax
import jax.numpy as jnp
from jax import lax
from jax.sharding import PartitionSpec as P

CHANNEL_DIM = 64


EPS = 1e-05
BETA = 0.9
HIGH_ACCURACY = lax.Precision.HIGHEST


def neighbour_attention(query_rows, key_rows, value_rows, listed):
    attention_logits = jnp.einsum(
        "yrw,lrw->ryl", query_rows, key_rows, precision=HIGH_ACCURACY
    ) * query_rows.shape[-1] ** (-0.5)
    present = listed[None] > 0.0
    masked = jnp.where(present, attention_logits, -1e30)
    highest = jnp.max(masked, axis=-1, keepdims=True)
    attention_probabilities = listed[None] * jnp.exp(masked - highest)
    attention_probabilities = attention_probabilities / jnp.sum(
        attention_probabilities, axis=-1, keepdims=True
    )
    return jnp.einsum("kcj,jkl->ckl", attention_probabilities, value_rows, precision=HIGH_ACCURACY)


def wgrad(left, right):
    return jnp.einsum("rd,rc->dc", left, right, preferred_element_type=jnp.float32)


def back_dot(grad, weight):
    return jnp.einsum("rc,dc->rd", grad, weight, preferred_element_type=jnp.float32)


def shards(
    node_input,
    cotangent,
    norm_gain,
    norm_bias,
    query_weight,
    key_weight,
    value_weight,
    gate_weight,
    out_weight,
    adjacent_vertices,
    active_vertex_tally,
    training_period,
):
    rows, column_ids = node_input.shape
    slots = active_vertex_tally.shape[0]
    nodes = rows // slots
    heads_here = column_ids // CHANNEL_DIM
    column_offset = lax.axis_index("head") * column_ids
    full, entire_norm_gain, complete_bias = (
        lax.all_gather(node_input, "head", axis=1, tiled=True),
        lax.all_gather(norm_gain, "head", axis=0, tiled=True),
        lax.all_gather(norm_bias, "head", axis=0, tiled=True),
    )
    whole = full.astype(jnp.float32)
    feature_mean = jnp.mean(whole, axis=-1, keepdims=True)
    centred_input = whole - feature_mean
    inverse_deviation = lax.rsqrt(
        jnp.mean(centred_input * centred_input, axis=-1, keepdims=True) + EPS
    )
    standardized = centred_input * inverse_deviation
    normed_input = (
        standardized * entire_norm_gain.astype(jnp.float32) + complete_bias.astype(jnp.float32)
    ).astype(jnp.bfloat16)
    query = jnp.dot(normed_input, query_weight, preferred_element_type=jnp.float32)
    key = jnp.dot(normed_input, key_weight, preferred_element_type=jnp.float32)
    value = jnp.dot(normed_input, value_weight, preferred_element_type=jnp.float32)
    gate = jnp.dot(normed_input, gate_weight, preferred_element_type=jnp.float32)
    adjacency_table = adjacent_vertices.reshape(slots, nodes, adjacent_vertices.shape[1])
    node_slots = jnp.arange(nodes, dtype=jnp.int32)
    listed_counts = jnp.sum(
        (adjacency_table[:, :, :, None] == node_slots[None, None, None, :]).astype(jnp.float32),
        axis=2,
    )

    def local_all(qq, kk, vv):
        regrouped_source = (slots, nodes, heads_here, CHANNEL_DIM)
        out = jax.vmap(neighbour_attention)(
            qq.reshape(regrouped_source),
            kk.reshape(regrouped_source),
            vv.reshape(regrouped_source),
            listed_counts,
        )
        return out.reshape(rows, column_ids)

    local_out, local_back = jax.vjp(local_all, query, key, value)
    active_vertex = (
        (node_slots[None, :] < active_vertex_tally[:, None]).reshape(rows).astype(jnp.float32)
    )
    retain_flag = (
        (1 - training_period).astype(jnp.float32)[:, None] * jnp.ones((1, nodes), jnp.float32)
    ).reshape(rows)
    q_pos = jax.nn.sigmoid(query).reshape(rows, heads_here, CHANNEL_DIM)
    k_sig = jax.nn.sigmoid(key).reshape(rows, heads_here, CHANNEL_DIM)
    k_pos = k_sig * active_vertex[:, None, None]
    vals = value.reshape(rows, heads_here, CHANNEL_DIM)
    summary = jnp.einsum("nha,nhb->hab", k_pos, vals, precision=HIGH_ACCURACY)
    key_total = jnp.sum(k_pos, axis=0)
    summary, key_total = lax.psum((summary, key_total), "graph")
    numer = jnp.einsum("nha,hab->nhb", q_pos, summary, precision=HIGH_ACCURACY)
    denom = jnp.einsum("nha,ha->nh", q_pos, key_total, precision=HIGH_ACCURACY)
    glob = numer / denom[..., None]
    attended = local_out + glob.reshape(rows, column_ids)
    mixed_low = ((1.0 - BETA) * gate * attended + BETA * attended).astype(jnp.bfloat16)
    mixed_full = lax.all_gather(mixed_low, "head", axis=1, tiled=True)
    layer_output = (
        node_input.astype(jnp.float32)
        + jnp.dot(mixed_full, out_weight, preferred_element_type=jnp.float32)
    ).astype(jnp.bfloat16)
    mixed_grad = lax.psum_scatter(
        back_dot(cotangent, out_weight), "head", scatter_dimension=1, tiled=True
    )
    out_wgrad = wgrad(mixed_full, cotangent)
    gate_back = mixed_grad * (1.0 - BETA) * attended
    att_grad = mixed_grad * ((1.0 - BETA) * gate + BETA)
    glob_grad = att_grad.reshape(rows, heads_here, CHANNEL_DIM) * retain_flag[:, None, None]
    numer_grad = glob_grad / denom[..., None]
    denom_grad = -jnp.sum(glob_grad * glob, axis=-1) / denom
    qpos_grad = (
        jnp.einsum("nhb,hab->nha", numer_grad, summary, precision=HIGH_ACCURACY)
        + denom_grad[..., None] * key_total[None]
    )
    summary_part = jnp.einsum("nha,nhb->hab", q_pos, numer_grad, precision=HIGH_ACCURACY)
    total_part = jnp.einsum("nh,nha->ha", denom_grad, q_pos, precision=HIGH_ACCURACY)
    summary_back, total_back = lax.psum((summary_part, total_part), "graph")
    kpos_grad = (
        jnp.einsum("hab,nhb->nha", summary_back, vals, precision=HIGH_ACCURACY) + total_back[None]
    )
    value_glob = jnp.einsum("nha,hab->nhb", k_pos, summary_back, precision=HIGH_ACCURACY)
    query_local, key_local, value_local = local_back(att_grad)
    query_back = (
        query_local + (qpos_grad * q_pos * (1.0 - q_pos)).reshape(rows, column_ids)
    ).astype(jnp.bfloat16)
    key_back = (
        key_local
        + (kpos_grad * active_vertex[:, None, None] * k_sig * (1.0 - k_sig)).reshape(
            rows, column_ids
        )
    ).astype(jnp.bfloat16)
    value_back = (value_local + value_glob.reshape(rows, column_ids)).astype(jnp.bfloat16)
    gate_low = gate_back.astype(jnp.bfloat16)
    query_wgrad = wgrad(normed_input, query_back)
    key_wgrad = wgrad(normed_input, key_back)
    value_wgrad = wgrad(normed_input, value_back)
    gate_wgrad = wgrad(normed_input, gate_low)
    normed_part = back_dot(query_back, query_weight) + back_dot(key_back, key_weight)
    normed_part = normed_part + back_dot(value_back, value_weight) + back_dot(gate_low, gate_weight)
    standardized_self = lax.dynamic_slice_in_dim(standardized, column_offset, column_ids, 1)
    normed_grad = lax.psum(normed_part, "head")
    scaled_input = normed_grad * entire_norm_gain.astype(jnp.float32)
    inner = inverse_deviation * (
        scaled_input
        - jnp.mean(scaled_input, axis=-1, keepdims=True)
        - standardized * jnp.mean(scaled_input * standardized, axis=-1, keepdims=True)
    )
    inner_own = lax.dynamic_slice_in_dim(inner, column_offset, column_ids, 1)
    self_gradient = lax.dynamic_slice_in_dim(normed_grad, column_offset, column_ids, 1)
    input_grad = (cotangent.astype(jnp.float32) + inner_own).astype(jnp.bfloat16)
    partial_gain = jnp.sum(self_gradient * standardized_self, axis=0)
    bias_part = jnp.sum(self_gradient, axis=0)
    summed = lax.psum(
        (partial_gain, bias_part, query_wgrad, key_wgrad, value_wgrad, gate_wgrad, out_wgrad),
        "graph",
    )
    return (
        layer_output,
        input_grad,
        summed[0],
        summed[1],
        summed[2],
        summed[3],
        summed[4],
        summed[5],
        summed[6],
    )


def solution(mesh):
    placed = (
        P("graph", "head"),
        P("graph", "head"),
        P("head"),
        P("head"),
        P(None, "head"),
        P(None, "head"),
        P(None, "head"),
        P(None, "head"),
        P(None, "head"),
        P("graph", None),
        P("graph"),
        P("graph"),
    )
    return jax.shard_map(
        shards,
        mesh=mesh,
        in_specs=placed,
        out_specs=(
            P("graph", "head"),
            P("graph", "head"),
            P("head"),
            P("head"),
            P(None, "head"),
            P(None, "head"),
            P(None, "head"),
            P(None, "head"),
            P(None, "head"),
        ),
        check_vma=False,
    )
```

profile of v0, /device:TPU:0, one launch (start us, length us, event | category | flops | bytes accessed | tf_op | source)
XLA Modules:
  0.0 507.8 jit_solution(5015377293469693720)
XLA Ops:
  8.5 3.7 fusion.79
  16.9 6.4 %convert_reduce_fusion = f32[16,128,128]{2,1,0:T(8,128)S(1)} fusion(s32[16,128,16]{2,1,0:T(8,128)S(1)} %bitcast.194), kind=kLoop, calls=%fused_computation | loop fusion | flops 12320768 | bytes 1179648 | tf_op jit(solution)/shard_map/reduce_sum | solution.py:76
  38.0 3.0 multiply_reduce_fusion.4
  41.1 43.9 %psum.85 = f32[4,64]{1,0:T(4,128)S(1)} all-reduce(f32[4,64]{1,0:T(4,128)S(1)} %reduce_sum.132), channel_id=1, replica_groups=mesh['graph'=16,'head'=2] {'graph'}, use_global_device_ids=true, to_apply=%region_7.8 | all-reduce | flops 256 | bytes 2048 | tf_op jit(solution)/shard_map/psum | solution.py:104
  85.0 2.8 fusion.78
  90.8 7.9 %fusion.76 = (f32[16,4,128]{2,1,0:T(4,128)S(1)}, f32[16,4,128,128]{2,3,1,0:T(8,128)S(1)}) fusion(f32[16,128,4,64]{1,0,3,2:T(8,128)S(1)} %bitcast.180, f32[16,128,4,64]{1,0,3,2:T(8,128)S(1)} %bitcast.178, pred[16,128,128]{1,2,0:T(8,128)(4,1)S(1)} %copy-done.29), kind=kOutput, calls=%fused_computation.113 | convolution fusion | flops 808443904 | bytes 8683520 | tf_op jit(solution)/shard_map/jvp(vmap(yrw,lrw->ryl))/dot_general | solution.py:15
  101.8 5.0 fusion.50
  106.8 2.6 copy.82
  109.5 2.8 fusion.48
  112.3 4.5 fusion.75
  119.7 10.0 %fusion.53 = f32[16,128,4,64]{1,3,2,0:T(8,128)} fusion(f32[16,128,4,64]{1,0,3,2:T(8,128)S(1)} %bitcast.198, f32[16,4,128,128]{2,3,1,0:T(8,128)S(1)} %copy-done.2, f32[16,4,128]{2,1,0:T(4,128)S(1)} %fusion.14, f32[16,4,128]{2,1,0:T(4,128)S(1)} %get-tuple-element.40, f32[16,128,128]{1,2,0:T(8,128)S(1)} %copy.76), kind=kOutput, calls=%fused_computation.85 | convolution fusion | flops 808452096 | bytes 9502720 | tf_op jit(solution)/shard_map/transpose(jvp(vmap(kcj,jkl->ckl)))/dot_general | solution.py:25
  129.8 11.2 %convert_reduce_fusion.2 = (f32[16,4,128]{2,1,0:T(4,128)}, pred[16,4,128,128]{2,3,1,0:T(32,128)(4,1)}, f32[16,4,128]{2,1,0:T(4,128)S(1)}, f32[16,4,128,128]{2,3,1,0:T(8,128)}) fusion(f32[16,4,128,128]{2,3,1,0:T(8,128)S(1)} %copy-done.2, f32[16,4,128]{2,1,0:T(4,128)S(1)} %get-tuple-element.40, f32[16,128,128]{1,2,0:T(8,128)S(1)} %copy.76, ...), kind=kOutput, calls=%fused_computation.10 | convolution fusion | flops 813678592 | bytes 14811136 | tf_op jit(solution)/shard_map/transpose(jvp(vmap(kcj,jkl->ckl)))/dot_general | solution.py:25
  141.0 2.8 fusion.64
  144.4 5.7 %fusion.74 = (f32[16,4,128]{2,1,0:T(4,128)S(1)}, f32[16,4,128,128]{2,3,1,0:T(8,128)S(1)}) fusion(f32[16,4,128,128]{2,3,1,0:T(8,128)} %copy-done.1, f32[16,4,128]{2,1,0:T(4,128)S(1)} %get-tuple-element.40, f32[16,4,128]{2,1,0:T(4,128)S(1)} %neg.20, f32[16,4,128,128]{2,3,1,0:T(8,128)} %get-tuple-element.42, f32[16,4,128]{2,1,0:T(4,128)S(1)} %fusion.14, ...), kind=kLoop, calls=%fused_computation.111 | loop fusion | flops 6283264 | bytes 13762560 | tf_op jit(solution)/shard_map/transpose(jvp(vmap()))/reduce_sum | solution.py:21
  150.2 9.1 %fusion.59 = f32[16,128,4,64]{1,3,2,0:T(8,128)S(1)} fusion(f32[16,128,4,64]{1,0,3,2:T(8,128)S(1)} %bitcast.179, f32[16,4,128,128]{2,3,1,0:T(8,128)S(1)} %get-tuple-element.24, pred[16,4,128,128]{2,3,1,0:T(32,128)(4,1)S(1)} %copy-done.28, f32[16,4,128]{2,1,0:T(4,128)S(1)} %bitcast.201, pred[16,128,128]{1,2,0:T(8,128)(4,1)S(1)} %copy-done.30), kind=kOutput, calls=%fused_computation.87 | convolution fusion | flops 809500672 | bytes 9732096 | tf_op jit(solution)/shard_map/transpose(jvp(vmap(yrw,lrw->ryl)))/dot_general | solution.py:15
  159.3 5.2 %fusion.56 = f32[16,128,4,64]{1,3,2,0:T(8,128)S(1)} fusion(f32[16,128,4,64]{1,0,3,2:T(8,128)S(1)} %bitcast.181, f32[16,4,128,128]{2,3,1,0:T(8,128)S(1)} %get-tuple-element.24, pred[16,4,128,128]{2,3,1,0:T(32,128)(4,1)S(1)} %copy-done.28, f32[16,4,128]{2,1,0:T(4,128)S(1)} %bitcast.202, pred[16,128,128]{1,2,0:T(8,128)(4,1)S(1)} %copy-done.30), kind=kOutput, calls=%fused_computation.86 | convolution fusion | flops 809500672 | bytes 9732096 | tf_op jit(solution)/shard_map/transpose(jvp(vmap(yrw,lrw->ryl)))/dot_general | solution.py:15
  164.5 2.6 copy.94
  167.1 2.6 copy.89
  172.3 74.8 %all-reduce.11.cloned.1.call-done = (f32[4,64,64]{2,1,0:T(8,128)}, f32[4,64,64]{2,1,0:T(8,128)}) async-done(((f32[4,64,64]{2,1,0:T(8,128)}, f32[4,64,64]{2,1,0:T(8,128)}), (f32[4,64,64]{2,1,0:T(8,128)}, f32[4,64,64]{2,1,0:T(8,128)})) %all-reduce.11.cloned.1.call-update) | async-done | bytes 131088 | tf_op jit(solution)/shard_map/psum | solution.py:104
  247.1 6.0 %multiply_reduce_fusion.3 = (f32[2048,4]{0,1:T(4,128)S(1)}, f32[2048,4,64]{0,2,1:T(8,128)}) fusion(f32[2048,256]{0,1:T(8,128)} %copy-done.19, f32[2048]{0:T(1024)S(1)} %copy-done.56, f32[2048,4]{0,1:T(4,128)S(1)} %bitcast.207, f32[4,64,64]{2,1,0:T(8,128)} %get-tuple-element.20, f32[2048,4,64]{0,2,1:T(8,128)} %bitcast.184), kind=kOutput, calls=%fused_computation.55 | convolution fusion | flops 404742144 | bytes 6430720 | tf_op jit(solution)/shard_map/nha,hab->nhb/dot_general | solution.py:105
  253.1 3.7 fusion.10
  258.6 40.0 %psum.87 = f32[4,64]{1,0:T(4,128)S(1)} all-reduce(f32[4,64]{1,0:T(4,128)S(1)} %bitcast.212), channel_id=1, replica_groups=mesh['graph'=16,'head'=2] {'graph'}, use_global_device_ids=true, to_apply=%region_14.15 | all-reduce | flops 256 | bytes 2048 | tf_op jit(solution)/shard_map/psum | solution.py:130
  298.6 6.0 %multiply_convert_fusion.1 = (bf16[2048,256]{0,1:T(8,128)(2,1)}, bf16[2048,256]{0,1:T(8,128)(2,1)}) fusion(f32[2048,256]{0,1:T(8,128)} %reduce-scatter.2.cloned.1.call-done, f32[2048,4,64]{0,2,1:T(8,128)} %get-tuple-element.44, f32[32,8,16,128]{3,2,1,0:T(8,128)} %bitcast.182, f32[2048,256]{0,1:T(8,128)} %get-tuple-element.39), kind=kLoop, calls=%fused_computation.54 | loop fusion | flops 3145728 | bytes 10485760 | tf_op jit(solution)/shard_map/convert_element_type | solution.py:146
  304.7 3.1 fusion.20
  318.9 2.8 add_add_fusion
  323.3 3.0 fusion.85
  331.0 3.4 fusion.87
  335.6 3.6 fusion.17
  339.1 7.1 %all-reduce.7.cloned.1.call-done = f32[2048,512]{1,0:T(8,128)} async-done(((f32[2048,512]{1,0:T(8,128)}), f32[2048,512]{1,0:T(8,128)}) %all-reduce.7.cloned.1.call-update) | async-done | bytes 4194320 | tf_op jit(solution)/shard_map/psum | solution.py:154
  346.2 4.0 fusion.73
  352.8 44.0 %all-reduce = (f32[256]{0:T(256)}, f32[256]{0:T(256)}) all-reduce(f32[256]{0:T(256)S(1)} %get-tuple-element.10, f32[256]{0:T(256)S(1)} %get-tuple-element.9), channel_id=1, replica_groups=mesh['graph'=16,'head'=2] {'graph'}, use_global_device_ids=true, to_apply=%region_19.20 | all-reduce | flops 512 | bytes 4096 | tf_op jit(solution)/shard_map/psum | solution.py:166
  396.7 97.7 %all-reduce.9.cloned.1.call-done = (f32[512,256]{1,0:T(8,128)}, f32[512,256]{1,0:T(8,128)}, f32[512,256]{1,0:T(8,128)}, f32[512,256]{1,0:T(8,128)}, f32[512,256]{1,0:T(8,128)}) async-done(((f32[512,256]{1,0:T(8,128)}, f32[512,256]{1,0:T(8,128)}, f32[512,256]{1,0:T(8,128)}, f32[512,256]{1,0:T(8,128)}, f32[512,256]{1,0:T(8,128)}), (f32[512,256]{1,0:T(8,128)}, f32[512,256]{1,0:T(8,128)}, f32[512,256]{1,0:T(8,128)}, ...) | async-done | bytes 2621456 | tf_op jit(solution)/shard_map/psum | solution.py:166
  (189 shorter events, 61.8 us)
Async XLA Ops:
  7.2 30.8 %copy-start = (bf16[512,256]{1,0:T(8,128)(2,1)S(1)}, bf16[512,256]{1,0:T(8,128)(2,1)}, u32[]{:S(2)}) copy-start(bf16[512,256]{1,0:T(8,128)(2,1)} %param.17) | copy-start | bytes 786436
  7.2 18.4 %all-gather.5.cloned.1.call-start = ((), (), s32[]{:S(2)}) async-start(), calls=%async_computation.1 | async-start | bytes 3145728 | tf_op jit(solution)/shard_map/all_gather | solution.py:56
  7.9 104.3 %reduce-scatter.2.cloned.1.call-start = ((), (), s32[]{:S(2)}) async-start(), calls=%async_computation.3 | async-start | bytes 6291456 | tf_op jit(solution)/shard_map/reduce_scatter | solution.py:115
  12.2 234.8 %all-reduce.11.cloned.1.call-start = ((), (), s32[]{:S(2)}) async-start(), calls=%async_computation.6 | async-start | bytes 524288 | tf_op jit(solution)/shard_map/psum | solution.py:104
  14.7 14.1 %copy-start.51 = (f32[2,1,256]{2,1,0:T(1,128)}, f32[2,1,256]{2,1,0:T(1,128)S(1)}, u32[]{:S(2)}) copy-start(f32[2,1,256]{2,1,0:T(1,128)S(1)} %convert_element_type.78) | copy-start | bytes 6148
  31.3 6.6 %copy-start.11 = (bf16[2048,512]{1,0:T(8,128)(2,1)}, bf16[2048,512]{1,0:T(8,128)(2,1)S(1)}, u32[]{:S(2)}) copy-start(bf16[2048,512]{1,0:T(8,128)(2,1)S(1)} %get-tuple-element.34) | copy-start | bytes 6291460
  88.9 9.8 %copy-start.9 = (f32[32,8,16,128]{3,2,1,0:T(8,128)}, f32[32,8,16,128]{3,2,1,0:T(8,128)S(1)}, u32[]{:S(2)}) copy-start(f32[32,8,16,128]{3,2,1,0:T(8,128)S(1)} %copy.110) | copy-start | bytes 6291460
  116.8 24.2 %copy-start.19 = (f32[2048,256]{0,1:T(8,128)}, f32[2048,256]{0,1:T(8,128)S(1)}, u32[]{:S(2)}) copy-start(f32[2048,256]{0,1:T(8,128)S(1)} %get-tuple-element.38) | copy-start | bytes 6291460
  119.7 10.0 %copy-start.33 = (f32[32,8,16,128]{3,2,1,0:T(8,128)S(1)}, f32[32,8,16,128]{3,2,1,0:T(8,128)}, u32[]{:S(2)}) copy-start(f32[32,8,16,128]{3,2,1,0:T(8,128)} %copy.108) | copy-start | bytes 6291460
  129.8 11.3 %copy-start.15 = (f32[2048,256]{0,1:T(8,128)S(1)}, f32[2048,256]{0,1:T(8,128)}, u32[]{:S(2)}) copy-start(f32[2048,256]{0,1:T(8,128)} %get-tuple-element.36) | copy-start | bytes 6291460
  129.8 11.3 %copy-start.49 = (f32[4,1,2048]{2,0,1:T(4,128)S(1)}, f32[4,1,2048]{2,0,1:T(4,128)}, u32[]{:S(2)}) copy-start(f32[4,1,2048]{2,0,1:T(4,128)} %copy.165) | copy-start | bytes 98308
  129.8 11.3 %copy-start.55 = (f32[2048]{0:T(1024)S(1)}, f32[2048]{0:T(1024)}, u32[]{:S(2)}) copy-start(f32[2048]{0:T(1024)} %broadcast_bitcast_fusion) | copy-start | bytes 24580
  143.9 187.1 %all-gather.7.cloned.1.call-start = ((), (), s32[]{:S(2)}) async-start(), calls=%async_computation.2 | async-start | bytes 3145728 | tf_op jit(solution)/shard_map/all_gather | solution.py:110
  144.4 5.8 %copy-start.48 = (f32[16,4,128]{2,1,0:T(4,128)S(1)}, f32[16,4,128]{2,1,0:T(4,128)}, u32[]{:S(2)}) copy-start(f32[16,4,128]{2,1,0:T(4,128)} %get-tuple-element.25) | copy-start | bytes 98308
  144.4 5.8 %copy-start.8 = (f32[32,8,16,128]{3,2,1,0:T(8,128)S(1)}, f32[32,8,16,128]{3,2,1,0:T(8,128)}, u32[]{:S(2)}) copy-start(f32[32,8,16,128]{3,2,1,0:T(8,128)} %copy.109) | copy-start | bytes 6291460
  144.4 5.8 %copy-start.28 = (pred[16,4,128,128]{2,3,1,0:T(32,128)(4,1)S(1)}, pred[16,4,128,128]{2,3,1,0:T(32,128)(4,1)}, u32[]{:S(2)}) copy-start(pred[16,4,128,128]{2,3,1,0:T(32,128)(4,1)} %get-tuple-element.26) | copy-start | bytes 3145732
  144.4 5.8 %copy-start.30 = (pred[16,128,128]{1,2,0:T(8,128)(4,1)S(1)}, pred[16,128,128]{1,2,0:T(8,128)(4,1)}, u32[]{:S(2)}) copy-start(pred[16,128,128]{1,2,0:T(8,128)(4,1)} %copy.77) | copy-start | bytes 786436
  150.2 9.1 %copy-start.10 = (f32[32,8,16,128]{3,2,1,0:T(8,128)S(1)}, f32[32,8,16,128]{3,2,1,0:T(8,128)}, u32[]{:S(2)}) copy-start(f32[32,8,16,128]{3,2,1,0:T(8,128)} %copy-done.9) | copy-start | bytes 6291460
  159.3 5.2 %copy-start.31 = (f32[16,128,4,64]{1,3,2,0:T(8,128)S(1)}, f32[16,128,4,64]{1,3,2,0:T(8,128)}, u32[]{:S(2)}) copy-start(f32[16,128,4,64]{1,3,2,0:T(8,128)} %fusion.53) | copy-start | bytes 6291460
  169.7 77.3 %copy-start.50 = (f32[4,1,2048]{2,0,1:T(4,128)S(1)}, f32[4,1,2048]{2,0,1:T(4,128)}, u32[]{:S(2)}) copy-start(f32[4,1,2048]{2,0,1:T(4,128)} %copy.165) | copy-start | bytes 98308
  169.7 77.3 %copy-start.56 = (f32[2048]{0:T(1024)S(1)}, f32[2048]{0:T(1024)}, u32[]{:S(2)}) copy-start(f32[2048]{0:T(1024)} %broadcast_bitcast_fusion) | copy-start | bytes 24580
  247.0 6.0 %copy-start.16 = (f32[2048,256]{0,1:T(8,128)S(1)}, f32[2048,256]{0,1:T(8,128)}, u32[]{:S(2)}) copy-start(f32[2048,256]{0,1:T(8,128)} %get-tuple-element.36) | copy-start | bytes 6291460
  247.0 6.0 %copy-start.20 = (f32[2048,256]{0,1:T(8,128)S(1)}, f32[2048,256]{0,1:T(8,128)}, u32[]{:S(2)}) copy-start(f32[2048,256]{0,1:T(8,128)} %copy-done.19) | copy-start | bytes 6291460
  247.0 6.0 %copy-start.54 = (f32[4,64]{1,0:T(4,128)S(1)}, f32[4,64]{1,0:T(4,128)}, u32[]{:S(2)}) copy-start(f32[4,64]{1,0:T(4,128)} %copy-done.53) | copy-start | bytes 3076
  247.1 6.0 %copy-start.58 = (f32[4,64,64]{2,1,0:T(8,128)S(1)}, f32[4,64,64]{2,1,0:T(8,128)}, u32[]{:S(2)}) copy-start(f32[4,64,64]{2,1,0:T(8,128)} %get-tuple-element.20) | copy-start | bytes 196612
  304.6 41.6 %all-reduce.7.cloned.1.call-start = ((), (), s32[]{:S(2)}) async-start(), calls=%async_computation.4 | async-start | bytes 8388608 | tf_op jit(solution)/shard_map/psum | solution.py:154
  321.8 172.7 %all-reduce.9.cloned.1.call-start = ((), (), s32[]{:S(2)}) async-start(), calls=%async_computation.5 | async-start | bytes 5242880 | tf_op jit(solution)/shard_map/psum | solution.py:166
  335.6 10.7 %copy-start.4 = (bf16[2048,512]{1,0:T(8,128)(2,1)S(1)}, bf16[2048,512]{1,0:T(8,128)(2,1)}, u32[]{:S(2)}) copy-start(bf16[2048,512]{1,0:T(8,128)(2,1)} %all-gather.5.cloned.1.call-done) | copy-start | bytes 6291460
  335.6 10.7 %copy-start.47 = (f32[2048]{0:T(1024)S(1)}, f32[2048]{0:T(1024)}, u32[]{:S(2)}) copy-start(f32[2048]{0:T(1024)} %copy-done.46) | copy-start | bytes 24580
  335.6 10.7 %copy-start.52 = (f32[2,1,256]{2,1,0:T(1,128)S(1)}, f32[2,1,256]{2,1,0:T(1,128)}, u32[]{:S(2)}) copy-start(f32[2,1,256]{2,1,0:T(1,128)} %copy-done.51) | copy-start | bytes 6148
  339.1 11.1 %copy-start.25 = (bf16[2048,256]{1,0:T(8,128)(2,1)S(1)}, bf16[2048,256]{1,0:T(8,128)(2,1)}, u32[]{:S(2)}) copy-start(bf16[2048,256]{1,0:T(8,128)(2,1)} %param.13) | copy-start | bytes 3145732
  494.4 5.5 %copy-start.40 = (f32[512,256]{1,0:T(8,128)S(1)}, f32[512,256]{1,0:T(8,128)}, u32[]{:S(2)}) copy-start(f32[512,256]{1,0:T(8,128)} %get-tuple-element.55) | copy-start | bytes 1572868
  (36 other events, 86.6 us)
Sparse Core Ops, SparseCore 0:
  9.6 13.0 all-gather.4
  24.9 13.2 reduce-scatter.1
  144.0 102.9 all-reduce.10
  304.8 6.4 all-gather.6
  321.9 24.2 all-reduce.6
  354.6 139.7 all-reduce.8
where the time goes:
time: 514 us; the launch traced here: 508 us
  waiting for transfers between devices  180 us (35%)
  blocking collectives  132 us (26%)
  matrix products  107 us (21%)
  local copies, waits for them, and re-layouts  37.7 us (7%)
  other arithmetic  35.5 us (7%)
  between operations  15 us (3%)
    psum x1, waiting for transfers between devices, shards(): lax.psum((partial_gain, bias_part, query_wgrad, key_wgrad, value_wgrad, g...  97.7 us
    psum x1, waiting for transfers between devices, shards(): summary, key_total = lax.psum((summary, key_total), 'graph')  74.8 us
    psum x1, blocking collectives, shards(): lax.psum((partial_gain, bias_part, query_wgrad, key_wgrad, value_wgrad, g...  44 us
    psum x1, blocking collectives, shards(): summary, key_total = lax.psum((summary, key_total), 'graph')  43.9 us
    psum x1, blocking collectives, shards(): summary_back, total_back = lax.psum((summary_part, total_part), 'graph')  40 us
    dot_general x3, matrix products, neighbour_attention(): jnp.einsum('kcj,jkl->ckl', attention_probabilities, value_rows, precision...  26.3 us
    unnamed x135, local copies, waits for them, and re-layouts  24.2 us
    dot_general x3, matrix products, neighbour_attention(): jnp.einsum('yrw,lrw->ryl', query_rows, key_rows, precision=HIGH_ACCURACY)  22.2 us
  transfers between devices with their start and end apart: 6, of which 3 were waited for; matrix products, arithmetic and copies ran while one was open for 22% of the time, Pallas kernels for 0%

commit v1 on v0

v1 whole, which is shorter than its diff:
```python
import functools

import jax
import jax.numpy as jnp
from jax import lax
from jax.experimental import pallas as pl
from jax.experimental.pallas import tpu as pltpu
from jax.sharding import PartitionSpec as P

EPS = 1e-05
BETA = 0.9
LOG2E = 1.4426950408889634
BF = jnp.bfloat16
F32 = jnp.float32
MESH = pl.DeviceIdType.MESH
NODES = 128
CHUNKS = 16
QUERY, KEY, VALUE, GATE, OUT = 0, 1, 2, 3, 4


def nn(a, b):
    return lax.dot_general(a, b, (((1,), (0,)), ((), ())), preferred_element_type=F32)


def nt(a, b):
    return lax.dot_general(a, b, (((1,), (1,)), ((), ())), preferred_element_type=F32)


def tn(a, b):
    return lax.dot_general(a, b, (((0,), (0,)), ((), ())), preferred_element_type=F32)


def split(a):
    high = a.astype(BF)
    return high, (a - high.astype(F32)).astype(BF)


def rows_cat(*parts):
    return jnp.concatenate(parts, axis=0)


def lanes_cat(*parts):
    return jnp.concatenate(parts, axis=1)


def block(start, size):
    return pl.ds(pl.multiple_of(start * size, size), size)


def layer_kernel(
    groups,
    x,
    c,
    gain,
    bias,
    wq,
    wk,
    wv,
    wg,
    wo,
    adjacent,
    tally,
    period,
    layer_out,
    input_grad,
    small_grad,
    fin,
    xo,
    co,
    gbs,
    gbo,
    woo,
    wall,
    normed,
    mean_keep,
    rstd_keep,
    q,
    k,
    v,
    g,
    dmix,
    datt,
    att,
    prob,
    dq,
    dk,
    dv,
    low4,
    mix,
    mixo,
    dn_own,
    dn_send,
    dn_recv,
    st_send,
    st_recv,
    sum_part,
    sum_recv,
    sum_red,
    sum_hi,
    sum_full,
    part,
    psend,
    precv,
    zpart,
    zrecv,
    hrecv,
    gb_part,
    gb_recv,
    gb_hi,
    core_sems,
    mix_sems,
    dn_sems,
    ar_sems,
    arh_sems,
    w_sems,
    wh_sems,
    gb_sems,
    gbh_sems,
):
    A, B, C = groups
    L = A * B
    R, W = x.shape
    NB = R // NODES
    PAIRS = W // 128
    me = lax.axis_index("graph")
    head = lax.axis_index("head")
    other = 1 - head
    lo = lax.rem(me, L)
    hi = me // L
    al = lax.rem(lo, A)
    bl = lo // A

    def dev(h_, b_, a_):
        return (h_ * L + b_ * A + a_, head)

    lo_peers = [(hi * L + lax.rem(lo + d, L), head) for d in range(1, L)]
    hi_peers = [(lax.rem(hi + d, C) * L + lo, head) for d in range(1, C)]
    a_peers = [(lax.rem(al + d, A), dev(hi, bl, lax.rem(al + d, A))) for d in range(1, A)]
    b_peers = [(lax.rem(bl + d, B), dev(hi, lax.rem(bl + d, B), al)) for d in range(1, B)]
    partner = (me, other)
    own_rows = block(head, W)
    oth_rows = block(other, W)

    def send(src, dst, sems, index, to):
        copy = pltpu.make_async_remote_copy(
            src_ref=src,
            dst_ref=dst,
            send_sem=sems.at[(0,) + index],
            recv_sem=sems.at[(1,) + index],
            device_id=to,
            device_id_type=MESH,
        )
        copy.start()
        return copy

    barrier = pltpu.get_barrier_semaphore()
    greeted = [partner] + lo_peers + hi_peers
    for to in greeted:
        pl.semaphore_signal(barrier, inc=1, device_id=to, device_id_type=MESH)

    for i, w in enumerate((wq, wk, wv, wg)):
        wall[0:W, i * W : (i + 1) * W] = w[own_rows, :]
        wall[W : 2 * W, i * W : (i + 1) * W] = w[oth_rows, :]
    gbs[0:8, :] = jnp.broadcast_to(gain[...].astype(F32), (8, W))
    gbs[8:16, :] = jnp.broadcast_to(bias[...].astype(F32), (8, W))
    pl.semaphore_wait(barrier, len(greeted))

    XC = 4
    CC = 2
    core_copies = [send(gbs, gbo, core_sems, (0,), partner)]
    for i in range(XC):
        piece = pl.ds(i * (R // XC), R // XC)
        core_copies.append(send(x.at[piece], xo.at[piece], core_sems, (1 + i,), partner))
    core_copies.append(send(wo.at[oth_rows], woo, core_sems, (1 + XC,), partner))
    for i in range(CC):
        piece = pl.ds(i * (R // CC), R // CC)
        core_copies.append(send(c.at[piece], co.at[piece], core_sems, (2 + XC + i,), partner))

    RB = 256
    NR = R // RB

    def own_dmix(b, _):
        r = block(b, RB)
        dmix[r, :] = nt(c[r, :], wo[own_rows, :])
        return 0

    lax.fori_loop(0, NR, own_dmix, 0)

    sum_part[...] = jnp.zeros_like(sum_part)
    core_copies[0].wait_recv()
    gain_own, bias_own = gbs[0:1, :], gbs[8:9, :]
    gain_oth, bias_oth = gbo[0:1, :], gbo[8:9, :]
    lane_half = lax.broadcasted_iota(jnp.int32, (1, 128), 1) < 64
    node_of = lax.broadcasted_iota(jnp.int32, (NODES, 128), 0)

    def live_mask(s):
        return node_of < tally[s]

    def norm_block(b, carry):
        r = block(b, RB)
        xa = x[r, :].astype(F32)
        xb = xo[r, :].astype(F32)
        mean = (
            jnp.sum(xa, axis=1, keepdims=True) + jnp.sum(xb, axis=1, keepdims=True)
        ) * (1.0 / (2 * W))
        xa = xa - mean
        xb = xb - mean
        var = (
            jnp.sum(xa * xa, axis=1, keepdims=True) + jnp.sum(xb * xb, axis=1, keepdims=True)
        ) * (1.0 / (2 * W))
        rstd = lax.rsqrt(var + EPS)
        mean_keep[r, :] = jnp.broadcast_to(mean, (RB, 128))
        rstd_keep[r, :] = jnp.broadcast_to(rstd, (RB, 128))
        na = (xa * rstd * gain_own + bias_own).astype(BF)
        nb = (xb * rstd * gain_oth + bias_oth).astype(BF)
        normed[r, 0:W] = na
        normed[r, W : 2 * W] = nb
        kv = nn(lanes_cat(na, nb), wall[:, W : 3 * W])
        kk = kv[:, 0:W]
        vv = kv[:, W : 2 * W]
        k[r, :] = kk
        v[r, :] = vv
        sums, totals = carry
        new_sums, new_totals = [], []
        for p in range(PAIRS):
            ls = slice(p * 128, (p + 1) * 128)
            sig = jax.nn.sigmoid(kk[:, ls])
            kp = rows_cat(
                *[
                    jnp.where(live_mask(b * (RB // NODES) + i), sig[i * NODES : (i + 1) * NODES], 0.0)
                    for i in range(RB // NODES)
                ]
            )
            new_sums.append(sums[p] + tn(kp.astype(BF), vv[:, ls].astype(BF)))
            new_totals.append(totals[p] + jnp.sum(kp, axis=0, keepdims=True))
        return tuple(new_sums), tuple(new_totals)

    def zero_sums():
        return (
            tuple(jnp.zeros((128, 128), F32) for _ in range(PAIRS)),
            tuple(jnp.zeros((1, 128), F32) for _ in range(PAIRS)),
        )

    carry = zero_sums()
    for i in range(XC):
        core_copies[1 + i].wait_recv()
        carry = lax.fori_loop(i * (NR // XC), (i + 1) * (NR // XC), norm_block, carry)

    def pack_sums(slot, carry):
        sums, totals = carry
        for p in range(PAIRS):
            packed = jnp.where(lane_half, sums[p][0:64], sums[p][64:128])
            for j in range(8):
                sum_part[slot, p * 8 + j, 0:8, :] = packed[j * 8 : (j + 1) * 8]
            for j in range(CHUNKS):
                sum_part[slot, j, 8 + p : 9 + p, :] = totals[p]

    PER = CHUNKS // L

    def ar_scatter(slot):
        mine = block(lo, PER)
        sum_recv[slot, pl.ds(lo, 1)] = sum_part[slot, mine].reshape((1,) + sum_part.shape[1:][:0] + (PER,) + sum_part.shape[2:])
        copies = []
        for d in range(1, L):
            to = lax.rem(lo + d, L)
            copies.append(
                send(
                    sum_part.at[slot, block(to, PER)],
                    sum_recv.at[slot, lo],
                    ar_sems,
                    (slot, 0, d - 1),
                    lo_peers[d - 1],
                )
            )
        return copies

    def ar_reduce(slot, copies):
        for cp in copies:
            cp.wait()
        total = sum_recv[slot, 0]
        for i in range(1, L):
            total = total + sum_recv[slot, i]
        if C > 1:
            sum_hi[slot, pl.ds(hi, 1)] = total[None]
            sum_red[slot] = total
            hc = [
                send(sum_red.at[slot], sum_hi.at[slot, hi], arh_sems, (slot, d - 1), hi_peers[d - 1])
                for d in range(1, C)
            ]
            for cp in hc:
                cp.wait()
            total = sum_hi[slot, 0]
            for i in range(1, C):
                total = total + sum_hi[slot, i]
        sum_red[slot] = total
        sum_full[slot, block(lo, PER)] = total[:, 0:8, :]
        return [
            send(
                sum_red.at[slot, :, pl.ds(0, 8)],
                sum_full.at[slot, block(lo, PER)],
                ar_sems,
                (slot, 1, d - 1),
                lo_peers[d - 1],
            )
            for d in range(1, L)
        ]

    def ar_result(slot, copies):
        for cp in copies:
            cp.wait()
        mats, totals = [], []
        for p in range(PAIRS):
            packed = rows_cat(*[sum_full[slot, p * 8 + j] for j in range(8)])
            mats.append(
                rows_cat(jnp.where(lane_half, packed, 0.0), jnp.where(lane_half, 0.0, packed))
            )
            totals.append(sum_red[slot, 0, 8 + p : 9 + p, :])
        return mats, totals

    pack_sums(0, carry)
    ar0 = ar_scatter(0)

    for cp in core_copies[1 + XC :]:
        cp.wait_recv()

    def gate_block(b, _):
        r = block(b, RB)
        n = normed[r, :]
        q[r, :] = nn(n, wall[:, 0:W])
        gg = nn(n, wall[:, 3 * W : 4 * W])
        g[r, :] = gg
        dm = dmix[r, :] + nt(co[r, :], woo[...])
        dmix[r, :] = dm
        datt[r, :] = dm * ((1.0 - BETA) * gg + BETA)
        return 0

    lax.fori_loop(0, NR, gate_block, 0)
    ar0 = ar_reduce(0, ar0)

    half_row = jnp.where(lane_half, 1.0, 0.0)
    half_a = jnp.broadcast_to(half_row, (NODES, 128)).astype(BF)
    half_b = jnp.broadcast_to(1.0 - half_row, (NODES, 128)).astype(BF)

    def apart(a):
        return rows_cat(a * half_a, a * half_b)

    def joined(a):
        return jnp.where(lane_half, a[0:NODES], a[NODES : 2 * NODES])

    def forward_block(s, _):
        r = block(s, NODES)
        listed = adjacent[:, r]
        count = jnp.zeros((NODES, NODES), F32)
        for j in range(listed.shape[0]):
            count = count + jnp.where(listed[j : j + 1, :] == node_of, 1.0, 0.0)
        weight = jnp.where(count > 0.0, jnp.log(jnp.maximum(count, 1.0)) * LOG2E, -1e30)
        weight = lanes_cat(weight, weight)
        for p in range(PAIRS):
            ls = slice(p * 128, (p + 1) * 128)
            qh, ql = split(q[r, ls] * (0.125 * LOG2E))
            kh, kl = split(k[r, ls])
            vh, vl = split(v[r, ls])
            qbh = apart(qh)
            score = nt(lanes_cat(kh, kl, kh), lanes_cat(qbh, qbh, apart(ql))) + weight
            e = jnp.exp2(score - jnp.max(score, axis=0, keepdims=True))
            pr = e * (1.0 / jnp.sum(e, axis=0, keepdims=True))
            ph, plow = split(pr)
            prob[s, p, 0] = ph
            prob[s, p, 1] = plow
            o = tn(
                rows_cat(ph, plow),
                rows_cat(lanes_cat(vh, vl), lanes_cat(vh, jnp.zeros_like(vh))),
            )
            att[r, ls] = joined(o[:, 0:128] + o[:, 128:256])
        return 0

    lax.fori_loop(0, NB, forward_block, 0)

    mats, totals = ar_result(0, ar0)
    square = (2, 128, 128)
    same_head = (lax.broadcasted_iota(jnp.int32, (128, 128), 0) < 64) == (
        lax.broadcasted_iota(jnp.int32, (128, 128), 1) < 64
    )
    ones_bd = jnp.where(same_head, 1.0, 0.0).astype(BF)
    num_w, den_w, back_w = [], [], []
    for p in range(PAIRS):
        sh, sl = split(mats[p])
        th, tl = split(jnp.where(same_head, jnp.broadcast_to(totals[p], (128, 128)), 0.0))
        num_w.append(lanes_cat(sh, sl))
        den_w.append(rows_cat(th, tl))
        back_w.append(lanes_cat(sh, sh, sl))

    def glob_block(s, carry):
        r = block(s, NODES)
        keep = (1 - period[s]).astype(F32)
        sums, tots = carry
        new_sums, new_tots = [], []
        for p in range(PAIRS):
            ls = slice(p * 128, (p + 1) * 128)
            qp = jax.nn.sigmoid(q[r, ls])
            qpb = qp.astype(BF)
            num = nn(qpb, num_w[p])
            den = nt(qpb, den_w[p])
            inv = 1.0 / (den[:, 0:128] + den[:, 128:256])
            glob = (num[:, 0:128] + num[:, 128:256]) * inv
            at = att[r, ls] + glob
            mix[r, ls] = ((1.0 - BETA) * g[r, ls] * at + BETA * at).astype(BF)
            low4[GATE, r, ls] = (dmix[r, ls] * (1.0 - BETA) * at).astype(BF)
            dnum = (keep * datt[r, ls]) * inv
            dh, dl = split(dnum)
            th, tl = split(dnum * glob)
            dden = -nn(lanes_cat(th, tl), rows_cat(ones_bd, ones_bd))
            dqp = nt(lanes_cat(dh, dl, dh), back_w[p]) + dden * totals[p]
            dq[r, ls] = dqp * qp * (1.0 - qp)
            new_sums.append(sums[p] + tn(qpb, dh))
            new_tots.append(tots[p] + jnp.sum(dden * qp, axis=0, keepdims=True))
        return tuple(new_sums), tuple(new_tots)

    carry = lax.fori_loop(0, NB, glob_block, zero_sums())
    pack_sums(1, carry)
    ar1 = ar_scatter(1)
    mix_copy = send(mix, mixo, mix_sems, (0,), partner)

    KB = 512

    def weight_grads(kinds):
        def step(i, _):
            r = block(i, KB)
            n = normed[r, :]
            for kind in kinds:
                got = tn(n, low4[kind, r, :])
                part[kind, own_rows, :] += got[0:W]
                part[kind, oth_rows, :] += got[W : 2 * W]
            return 0

        for kind in kinds:
            part[kind] = jnp.zeros(part.shape[1:], F32)
        lax.fori_loop(0, R // KB, step, 0)

    def out_grads():
        def step(i, _):
            r = block(i, KB)
            cc = c[r, :]
            part[OUT, own_rows, :] += tn(mix[r, :], cc)
            part[OUT, oth_rows, :] += tn(mixo[r, :], cc)
            return 0

        part[OUT] = jnp.zeros(part.shape[1:], F32)
        lax.fori_loop(0, R // KB, step, 0)

    D = 2 * W
    PA = D // A
    PB = PA // B

    def w_scatter(w):
        psend[w] = part[w].astype(BF)
        return [
            send(psend.at[w, block(to, PA)], precv.at[w, i], w_sems, (w, 0, i), dv_)
            for i, (to, dv_) in enumerate(a_peers)
        ]

    def w_middle(w, copies):
        for cp in copies:
            cp.wait()
        total = part[w, block(al, PA), :]
        for i in range(A - 1):
            total = total + precv[w, i].astype(F32)
        zpart[w] = total
        return [
            send(zpart.at[w, block(to, PB)], zrecv.at[w, i], w_sems, (w, 1, i), dv_)
            for i, (to, dv_) in enumerate(b_peers)
        ]

    def w_spread(w, copies):
        for cp in copies:
            cp.wait()
        total = zpart[w, block(bl, PB), :]
        for i in range(B - 1):
            total = total + zrecv[w, i]
        here = pl.ds(pl.multiple_of(al * PA + bl * PB, PB), PB)
        if C > 1:
            hrecv[w, pl.ds(hi, 1)] = total[None]
            zpart[w, block(bl, PB), :] = total
            hc = [
                send(
                    zpart.at[w, block(bl, PB)], hrecv.at[w, hi], wh_sems, (w, d - 1), hi_peers[d - 1]
                )
                for d in range(1, C)
            ]
            for cp in hc:
                cp.wait()
            total = hrecv[w, 0]
            for i in range(1, C):
                total = total + hrecv[w, i]
        fin[w, here, :] = total.astype(BF)
        return [
            send(fin.at[w, here], fin.at[w, here], w_sems, (w, 2, i), dv_)
            for i, (_, dv_) in enumerate(b_peers)
        ]

    def w_gather(w, copies):
        for cp in copies:
            cp.wait()
        here = block(al, PA)
        return [
            send(fin.at[w, here], fin.at[w, here], w_sems, (w, 3, i), dv_)
            for i, (_, dv_) in enumerate(a_peers)
        ]

    def w_end(copies):
        for cp in copies:
            cp.wait()

    weight_grads((GATE,))
    gate_copies = w_scatter(GATE)
    mix_copy.wait_recv()
    out_grads()
    out_copies = w_scatter(OUT)

    def backward_block(s, _):
        r = block(s, NODES)
        for p in range(PAIRS):
            ls = slice(p * 128, (p + 1) * 128)
            qh, ql = split(q[r, ls])
            kh, kl = split(k[r, ls])
            vh, vl = split(v[r, ls])
            oh, ol = split(datt[r, ls])
            qbh, qbl = apart(qh), apart(ql)
            obh, obl = apart(oh), apart(ol)
            ph = prob[s, p, 0]
            plow = prob[s, p, 1]
            pr = ph.astype(F32) + plow.astype(F32)
            dp = nt(lanes_cat(vh, vl, vh), lanes_cat(obh, obh, obl))
            ds = pr * (dp - jnp.sum(pr * dp, axis=0, keepdims=True)) * 0.125
            dsh, dsl = split(ds)
            got = nn(ph, lanes_cat(obh, obl))
            dv[r, ls] = got[:, 0:128] + got[:, 128:256] + nn(plow, obh)
            got = nn(dsh, lanes_cat(qbh, qbl))
            dk[r, ls] = got[:, 0:128] + got[:, 128:256] + nn(dsl, qbh)
            got = tn(
                rows_cat(dsh, dsl),
                rows_cat(lanes_cat(kh, kl), lanes_cat(kh, jnp.zeros_like(kh))),
            )
            low4[QUERY, r, ls] = (dq[r, ls] + joined(got[:, 0:128] + got[:, 128:256])).astype(BF)
        return 0

    FIRST = NB // 2
    lax.fori_loop(0, FIRST, backward_block, 0)
    ar1 = ar_reduce(1, ar1)
    gate_copies = w_middle(GATE, gate_copies)
    out_copies = w_middle(OUT, out_copies)
    lax.fori_loop(FIRST, NB, backward_block, 0)
    gate_copies = w_spread(GATE, gate_copies)
    out_copies = w_spread(OUT, out_copies)
    weight_grads((QUERY,))
    query_copies = w_scatter(QUERY)
    gate_copies = w_gather(GATE, gate_copies)
    out_copies = w_gather(OUT, out_copies)

    mats, totals = ar_result(1, ar1)
    dsum = [m.astype(BF) for m in mats]

    def key_block(s, _):
        r = block(s, NODES)
        mask = live_mask(s)
        for p in range(PAIRS):
            ls = slice(p * 128, (p + 1) * 128)
            sig = jax.nn.sigmoid(k[r, ls])
            kp = jnp.where(mask, sig, 0.0)
            dkp = nt(v[r, ls].astype(BF), dsum[p]) + totals[p]
            low4[KEY, r, ls] = (dk[r, ls] + dkp * kp * (1.0 - sig)).astype(BF)
            low4[VALUE, r, ls] = (dv[r, ls] + nn(kp.astype(BF), dsum[p])).astype(BF)
        return 0

    lax.fori_loop(0, NB, key_block, 0)
    weight_grads((KEY, VALUE))
    key_copies = w_scatter(KEY)
    value_copies = w_scatter(VALUE)
    query_copies = w_middle(QUERY, query_copies)

    def normed_block(b, _):
        r = block(b, RB)
        grads = lanes_cat(*[low4[kind, r, :] for kind in (QUERY, KEY, VALUE, GATE)])
        dn = nt(grads, wall[...])
        dn_own[r, :] = dn[:, 0:W]
        dn_send[r, :] = dn[:, W : 2 * W]
        mean = mean_keep[r, 0:1]
        rstd = rstd_keep[r, 0:1]
        sa = dn[:, 0:W] * gain_own
        sb = dn[:, W : 2 * W] * gain_oth
        ha = (x[r, :].astype(F32) - mean) * rstd
        hb = (xo[r, :].astype(F32) - mean) * rstd
        s1 = jnp.sum(sa, axis=1, keepdims=True) + jnp.sum(sb, axis=1, keepdims=True)
        s2 = jnp.sum(sa * ha, axis=1, keepdims=True) + jnp.sum(sb * hb, axis=1, keepdims=True)
        st_send[r, :] = jnp.where(lane_half, s1, s2)
        return 0

    DC = 4
    dn_copies = []
    for i in range(DC):
        lax.fori_loop(i * (NR // DC), (i + 1) * (NR // DC), normed_block, 0)
        piece = pl.ds(i * (R // DC), R // DC)
        dn_copies.append(
            (
                send(dn_send.at[piece], dn_recv.at[piece], dn_sems, (0, i), partner),
                send(st_send.at[piece], st_recv.at[piece], dn_sems, (1, i), partner),
            )
        )
    query_copies = w_spread(QUERY, query_copies)
    key_copies = w_middle(KEY, key_copies)
    value_copies = w_middle(VALUE, value_copies)

    def out_block(b, _):
        r = block(b, RB)
        got = nn(mix[r, :], wo[own_rows, :]) + nn(mixo[r, :], wo[oth_rows, :])
        layer_out[r, :] = (x[r, :].astype(F32) + got).astype(BF)
        return 0

    lax.fori_loop(0, NR, out_block, 0)
    query_copies = w_gather(QUERY, query_copies)
    key_copies = w_spread(KEY, key_copies)
    value_copies = w_spread(VALUE, value_copies)

    def input_block(b, carry):
        gain_sum, bias_sum = carry
        r = block(b, RB)
        dn = dn_own[r, :] + dn_recv[r, :]
        st = st_send[r, :] + st_recv[r, :]
        mean = mean_keep[r, 0:1]
        rstd = rstd_keep[r, 0:1]
        s1 = st[:, 0:1] * (1.0 / (2 * W))
        s2 = st[:, 64:65] * (1.0 / (2 * W))
        ha = (x[r, :].astype(F32) - mean) * rstd
        inner = rstd * (dn * gain_own - s1 - ha * s2)
        input_grad[r, :] = (c[r, :].astype(F32) + inner).astype(BF)
        return (
            gain_sum + jnp.sum(dn * ha, axis=0, keepdims=True),
            bias_sum + jnp.sum(dn, axis=0, keepdims=True),
        )

    carry = (jnp.zeros((1, W), F32), jnp.zeros((1, W), F32))
    for i in range(DC):
        for cp in dn_copies[i]:
            cp.wait_recv()
        carry = lax.fori_loop(i * (NR // DC), (i + 1) * (NR // DC), input_block, carry)

    row = lax.broadcasted_iota(jnp.int32, (8, W), 0)
    terms = jnp.where(row == 0, carry[0], jnp.where(row == 1, carry[1], 0.0))
    gb_part[...] = terms
    gb_recv[pl.ds(lo, 1)] = terms[None]
    gb_copies = [
        send(gb_part, gb_recv.at[lo], gb_sems, (d - 1,), lo_peers[d - 1]) for d in range(1, L)
    ]
    key_copies = w_gather(KEY, key_copies)
    value_copies = w_gather(VALUE, value_copies)
    for cp in gb_copies:
        cp.wait()
    total = gb_recv[0]
    for i in range(1, L):
        total = total + gb_recv[i]
    if C > 1:
        gb_part[...] = total
        gb_hi[pl.ds(hi, 1)] = total[None]
        hc = [send(gb_part, gb_hi.at[hi], gbh_sems, (d - 1,), hi_peers[d - 1]) for d in range(1, C)]
        for cp in hc:
            cp.wait()
        total = gb_hi[0]
        for i in range(1, C):
            total = total + gb_hi[i]
    small_grad[...] = total
    for copies in (gate_copies, out_copies, query_copies, key_copies, value_copies):
        w_end(copies)
    for cp in core_copies:
        cp.wait_send()
    mix_copy.wait_send()
    for pair in dn_copies:
        for cp in pair:
            cp.wait_send()


def shards(
    groups,
    node_input,
    cotangent,
    norm_gain,
    norm_bias,
    query_weight,
    key_weight,
    value_weight,
    gate_weight,
    out_weight,
    adjacent_vertices,
    active_vertex_tally,
    training_period,
):
    A, B, C = groups
    L = A * B
    R, W = node_input.shape
    D = 2 * W
    NB = R // NODES
    PAIRS = W // 128
    PER = CHUNKS // L
    PA = D // A
    PB = PA // B
    VM = pltpu.VMEM
    dma = pltpu.SemaphoreType.DMA
    vmem = pl.BlockSpec(memory_space=pltpu.VMEM)
    smem = pl.BlockSpec(memory_space=pltpu.SMEM)
    layer_output, input_grad, small, fin = pl.pallas_call(
        functools.partial(layer_kernel, groups),
        name="layer_kernel",
        out_shape=(
            jax.ShapeDtypeStruct((R, W), BF),
            jax.ShapeDtypeStruct((R, W), BF),
            jax.ShapeDtypeStruct((8, W), F32),
            jax.ShapeDtypeStruct((5, D, W), BF),
        ),
        in_specs=[vmem] * 10 + [smem] * 2,
        out_specs=(vmem, vmem, vmem, vmem),
        scratch_shapes=[
            VM((R, W), BF),
            VM((R, W), BF),
            VM((16, W), F32),
            VM((16, W), F32),
            VM((W, W), BF),
            VM((D, 4 * W), BF),
            VM((R, D), BF),
            VM((R, 128), F32),
            VM((R, 128), F32),
            VM((R, W), F32),
            VM((R, W), F32),
            VM((R, W), F32),
            VM((R, W), F32),
            VM((R, W), F32),
            VM((R, W), F32),
            VM((R, W), F32),
            VM((NB, PAIRS, 2, NODES, 2 * NODES), BF),
            VM((R, W), F32),
            VM((R, W), F32),
            VM((R, W), F32),
            VM((4, R, W), BF),
            VM((R, W), BF),
            VM((R, W), BF),
            VM((R, W), F32),
            VM((R, W), F32),
            VM((R, W), F32),
            VM((R, 128), F32),
            VM((R, 128), F32),
            VM((2, CHUNKS, 16, 128), F32),
            VM((2, L, PER, 16, 128), F32),
            VM((2, PER, 16, 128), F32),
            VM((2, C, PER, 16, 128), F32),
            VM((2, CHUNKS, 8, 128), F32),
            VM((5, D, W), F32),
            VM((5, D, W), BF),
            VM((5, A - 1, PA, W), BF),
            VM((5, PA, W), F32),
            VM((5, B - 1, PB, W), F32),
            VM((5, C, PB, W), F32),
            VM((8, W), F32),
            VM((L, 8, W), F32),
            VM((C, 8, W), F32),
            dma((2, 8)),
            dma((2, 1)),
            dma((2, 2, 4)),
            dma((2, 2, 2, L - 1)),
            dma((2, 2, max(C - 1, 1))),
            dma((2, 5, 4, max(A, B) - 1)),
            dma((2, 5, max(C - 1, 1))),
            dma((2, L - 1)),
            dma((2, max(C - 1, 1))),
        ],
        compiler_params=pltpu.CompilerParams(
            collective_id=0, has_side_effects=True, vmem_limit_bytes=63 << 20
        ),
    )(
        node_input,
        cotangent,
        norm_gain.reshape(1, W),
        norm_bias.reshape(1, W),
        query_weight,
        key_weight,
        value_weight,
        gate_weight,
        out_weight,
        adjacent_vertices.T,
        active_vertex_tally,
        training_period,
    )
    full = fin.astype(F32)
    return (
        layer_output,
        input_grad,
        small[0],
        small[1],
        full[QUERY],
        full[KEY],
        full[VALUE],
        full[GATE],
        full[OUT],
    )


def factors(count):
    a = 4 if count % 4 == 0 else count
    b = 4 if count % (a * 4) == 0 else count // a
    return a, b, count // (a * b)


def solution(mesh):
    rows = P("graph", "head")
    cols = P(None, "head")
    return jax.shard_map(
        functools.partial(shards, factors(mesh.shape["graph"])),
        mesh=mesh,
        in_specs=(rows, rows, P("head"), P("head"))
        + (cols,) * 5
        + (P("graph", None), P("graph"), P("graph")),
        out_specs=(rows, rows, P("head"), P("head")) + (cols,) * 5,
        check_vma=False,
    )
```

time: 514 us -> 114 us (0.22); the launches traced: 508 us -> 114 us
  waiting for transfers between devices: 180 us -> 0 us
  blocking collectives: 132 us -> 0 us
  matrix products: 107 us -> 0 us
  Pallas kernels: 0 us -> 104 us
  other arithmetic: 35.5 us -> 1.55 us
  local copies, waits for them, and re-layouts: 37.7 us -> 7.55 us
  between operations: 15 us -> 0.68 us
    psum x3 -> x0, waiting for transfers between devices: 180 us -> none  [the longest x1 97.7 us: shards(): lax.psum((partial_gain, bias_part, query_wgrad, key_wgrad, value_wgrad, g...]
    psum x3 -> x0, blocking collectives: 128 us -> none  [the longest x1 44 us: shards(): lax.psum((partial_gain, bias_part, query_wgrad, key_wgrad, value_wgrad, g...]
    dot_general x29 -> x0, matrix products: 107 us -> none  [the longest x3 26.3 us: neighbour_attention(): jnp.einsum('kcj,jkl->ckl', attention_probabilities, value_rows, precision...]
    pallas_call x0 -> x1, Pallas kernels: none -> 104 us  [shards(): pl.pallas_call(functools.partial(layer_kernel, groups), name='layer_kerne...]
    reduce_sum x7 -> x0, other arithmetic: 22.2 us -> none  [the longest x1 6.38 us: shards(): jnp.sum((adjacency_table[:, :, :, None] == node_slots[None, None, None, :...]
    unnamed x135 -> x6, local copies, waits for them, and re-layouts: 24.2 us -> 2.25 us
    transpose x4 -> x0, local copies, waits for them, and re-layouts: 10.4 us -> none  [the longest x2 5.21 us: neighbour_attention(): jnp.einsum('kcj,jkl->ckl', attention_probabilities, value_rows, precision...]
    convert_element_type x8 -> x1, other arithmetic: 10.7 us -> 1.55 us  [shards(): full = fin.astype(F32)]
  transfers between devices with their start and end apart: 6 -> 0, of which waited for: 3 -> 0; matrix products, arithmetic and copies ran while one was open for 22% -> 0% of each run, Pallas kernels for 0% -> 0%
where the time goes in v1:
time: 114 us
  Pallas kernels  104 us (91%)
  local copies, waits for them, and re-layouts  7.55 us (7%)
  other arithmetic  1.55 us (1%)
    pallas_call x1, Pallas kernels, shards(): pl.pallas_call(functools.partial(layer_kernel, groups), name='layer_kerne...  104 us

profile of v1, /device:TPU:0, one launch (start us, length us, event | category | flops | bytes accessed | tf_op | source)
XLA Modules:
  0.0 113.7 jit_solution(14385777941458719037)
XLA Ops:
  0.6 1.2 %reshape.24.gain = bf16[1,256]{1,0:T(2,128)(2,1)} reshape(bf16[256]{0:T(256)(128)(2,1)} %param.14) | data formatting | bytes 1024 | tf_op jit(solution)/shard_map/reshape | solution.py:779
  1.9 1.2 %reshape.25.bias = bf16[1,256]{1,0:T(2,128)(2,1)} reshape(bf16[256]{0:T(256)(128)(2,1)} %param.15) | data formatting | bytes 1024 | tf_op jit(solution)/shard_map/reshape | solution.py:780
  3.1 103.9 %layer_kernel.1 = (bf16[2048,256]{1,0:T(8,128)(2,1)}, bf16[2048,256]{1,0:T(8,128)(2,1)}, f32[8,256]{1,0:T(8,128)}, bf16[5,512,256]{2,1,0:T(8,128)(2,1)}) custom-call(bf16[2048,256]{1,0:T(8,128)(2,1)} %x.1, bf16[2048,256]{1,0:T(8,128)(2,1)} %c.1, bf16[1,256]{1,0:T(2,128)(2,1)} %reshape.24.gain, bf16[1,256]{1,0:T(2,128)(2,1)} %reshape.25.bias, ...), custom_call_target="tpu_custom_call" | custom-call | tf_op jit(solution)/shard_map/layer_kernel/pallas_call | solution.py:709
  107.0 1.3 %fusion = (f32[1,256]{1,0:T(1,128)}, f32[1,256]{1,0:T(1,128)}) fusion(f32[8,256]{1,0:T(8,128)} %get-tuple-element.15), kind=kLoop, calls=%fused_computation.5 | loop fusion | bytes 4096 | tf_op jit(solution)/shard_map/slice | solution.py:795
  108.4 1.6 %convert_element_type.3 = f32[5,512,256]{2,1,0:T(8,128)S(1)} convert(bf16[5,512,256]{2,1,0:T(8,128)(2,1)} %get-tuple-element.16) | non-fusion elementwise | flops 655360 | bytes 3932160 | tf_op jit(solution)/shard_map/convert_element_type | solution.py:790
  109.9 0.0 copy-start.1
  109.9 0.0 copy-start
  109.9 1.5 %slice_bitcast_fusion = (f32[512,256]{1,0:T(8,128)}, f32[512,256]{1,0:T(8,128)}, f32[512,256]{1,0:T(8,128)}, f32[512,256]{1,0:T(8,128)}, f32[512,256]{1,0:T(8,128)}) fusion(f32[5,512,256]{2,1,0:T(8,128)S(1)} %convert_element_type.3), kind=kLoop, calls=%fused_computation | loop fusion | bytes 5242880 | tf_op jit(solution)/shard_map/squeeze | solution.py:800
  111.5 0.3 copy-done.1
  111.8 1.0 copy.23
  112.7 0.0 copy-done
  112.7 1.0 copy.24
Async XLA Ops:
  109.9 1.8 %copy-start.1 = (bf16[2048,256]{1,0:T(8,128)(2,1)S(1)}, bf16[2048,256]{1,0:T(8,128)(2,1)}, u32[]{:S(2)}) copy-start(bf16[2048,256]{1,0:T(8,128)(2,1)} %get-tuple-element.33) | copy-start | bytes 3145732
  109.9 2.8 %copy-start = (bf16[2048,256]{1,0:T(8,128)(2,1)S(1)}, bf16[2048,256]{1,0:T(8,128)(2,1)}, u32[]{:S(2)}) copy-start(bf16[2048,256]{1,0:T(8,128)(2,1)} %get-tuple-element.34) | copy-start | bytes 3145732

commit v2 on v1

--- a/solution.py
+++ b/solution.py
@@ -49,24 +49,30 @@
 
 def layer_kernel(
     groups,
-    x,
-    c,
+    x_hbm,
+    c_hbm,
     gain,
     bias,
     wq,
     wk,
     wv,
     wg,
-    wo,
-    adjacent,
+    wo_hbm,
+    adjacent_hbm,
     tally,
     period,
     layer_out,
     input_grad,
-    small_grad,
+    gain_grad,
+    bias_grad,
+    fin_hbm,
+    x,
+    xo,
+    c,
+    co,
+    wo,
+    adjacent,
     fin,
-    xo,
-    co,
     gbs,
     gbo,
     woo,
@@ -74,22 +80,23 @@
     normed,
     mean_keep,
     rstd_keep,
-    q,
-    k,
-    v,
+    q_sig,
+    k_sig,
+    qh,
+    ql,
+    kh,
+    kl,
+    vh,
+    vl,
     g,
     dmix,
     datt,
     att,
     prob,
     dq,
-    dk,
-    dv,
     low4,
     mix,
     mixo,
-    dn_own,
-    dn_send,
     dn_recv,
     st_send,
     st_recv,
@@ -107,6 +114,8 @@
     gb_part,
     gb_recv,
     gb_hi,
+    load_sems,
+    store_sems,
     core_sems,
     mix_sems,
     dn_sems,
@@ -153,25 +162,55 @@
         copy.start()
         return copy
 
+    dk, dv, dn_own, dn_send = att, q_sig, g, dmix
+
     barrier = pltpu.get_barrier_semaphore()
     greeted = [partner] + lo_peers + hi_peers
     for to in greeted:
         pl.semaphore_signal(barrier, inc=1, device_id=to, device_id_type=MESH)
 
-    for i, w in enumerate((wq, wk, wv, wg)):
-        wall[0:W, i * W : (i + 1) * W] = w[own_rows, :]
-        wall[W : 2 * W, i * W : (i + 1) * W] = w[oth_rows, :]
-    gbs[0:8, :] = jnp.broadcast_to(gain[...].astype(F32), (8, W))
-    gbs[8:16, :] = jnp.broadcast_to(bias[...].astype(F32), (8, W))
+    loads = []
+
+    def load(src, dst):
+        copy = pltpu.make_async_copy(src, dst, load_sems.at[len(loads)])
+        copy.start()
+        loads.append(copy)
+        return copy
+
+    XC = 4
+    x_loads = []
+    for i in range(XC):
+        piece = pl.ds(i * (R // XC), R // XC)
+        x_loads.append(load(x_hbm.at[piece], x.at[piece]))
+    wo_load = load(wo_hbm, wo)
+    c_load = load(c_hbm, c)
+    w_loads = []
+    for i, w in ((1, wk), (2, wv), (0, wq), (3, wg)):
+        cols = pl.ds(i * W, W)
+        w_loads.append(load(w.at[own_rows], wall.at[pl.ds(0, W), cols]))
+        w_loads.append(load(w.at[oth_rows], wall.at[pl.ds(W, W), cols]))
+    adjacent_load = load(adjacent_hbm, adjacent)
+
+    stores = []
+
+    def store(src, dst):
+        copy = pltpu.make_async_copy(src, dst, store_sems.at[len(stores)])
+        copy.start()
+        stores.append(copy)
+
+    gbs[0:8, :] = jnp.broadcast_to(gain[...].astype(F32).reshape(1, W), (8, W))
+    gbs[8:16, :] = jnp.broadcast_to(bias[...].astype(F32).reshape(1, W), (8, W))
     pl.semaphore_wait(barrier, len(greeted))
 
-    XC = 4
     CC = 2
     core_copies = [send(gbs, gbo, core_sems, (0,), partner)]
     for i in range(XC):
         piece = pl.ds(i * (R // XC), R // XC)
+        x_loads[i].wait()
         core_copies.append(send(x.at[piece], xo.at[piece], core_sems, (1 + i,), partner))
+    wo_load.wait()
     core_copies.append(send(wo.at[oth_rows], woo, core_sems, (1 + XC,), partner))
+    c_load.wait()
     for i in range(CC):
         piece = pl.ds(i * (R // CC), R // CC)
         core_copies.append(send(c.at[piece], co.at[piece], core_sems, (2 + XC + i,), partner))
@@ -193,8 +232,14 @@
     lane_half = lax.broadcasted_iota(jnp.int32, (1, 128), 1) < 64
     node_of = lax.broadcasted_iota(jnp.int32, (NODES, 128), 0)
 
-    def live_mask(s):
-        return node_of < tally[s]
+    def live_rows(first, a, count):
+        node = lax.broadcasted_iota(jnp.int32, (NODES, a.shape[1]), 0)
+        return rows_cat(
+            *[
+                jnp.where(node < tally[first + i], a[i * NODES : (i + 1) * NODES], 0.0)
+                for i in range(count)
+            ]
+        )
 
     def norm_block(b, carry):
         r = block(b, RB)
@@ -218,21 +263,20 @@
         kv = nn(lanes_cat(na, nb), wall[:, W : 3 * W])
         kk = kv[:, 0:W]
         vv = kv[:, W : 2 * W]
-        k[r, :] = kk
-        v[r, :] = vv
+        kh[r, :], kl[r, :] = split(kk)
+        vbf, vlow = split(vv)
+        vh[r, :] = vbf
+        vl[r, :] = vlow
+        sig = jax.nn.sigmoid(kk)
+        k_sig[r, :] = sig
+        kp = live_rows(b * (RB // NODES), sig, RB // NODES)
+        kpb = kp.astype(BF)
         sums, totals = carry
         new_sums, new_totals = [], []
         for p in range(PAIRS):
             ls = slice(p * 128, (p + 1) * 128)
-            sig = jax.nn.sigmoid(kk[:, ls])
-            kp = rows_cat(
-                *[
-                    jnp.where(live_mask(b * (RB // NODES) + i), sig[i * NODES : (i + 1) * NODES], 0.0)
-                    for i in range(RB // NODES)
-                ]
-            )
-            new_sums.append(sums[p] + tn(kp.astype(BF), vv[:, ls].astype(BF)))
-            new_totals.append(totals[p] + jnp.sum(kp, axis=0, keepdims=True))
+            new_sums.append(sums[p] + tn(kpb[:, ls], vbf[:, ls]))
+            new_totals.append(totals[p] + jnp.sum(kp[:, ls], axis=0, keepdims=True))
         return tuple(new_sums), tuple(new_totals)
 
     def zero_sums():
@@ -241,6 +285,8 @@
             tuple(jnp.zeros((1, 128), F32) for _ in range(PAIRS)),
         )
 
+    for cp in w_loads[0:4]:
+        cp.wait()
     carry = zero_sums()
     for i in range(XC):
         core_copies[1 + i].wait_recv()
@@ -320,13 +366,17 @@
     pack_sums(0, carry)
     ar0 = ar_scatter(0)
 
+    for cp in w_loads[4:]:
+        cp.wait()
     for cp in core_copies[1 + XC :]:
         cp.wait_recv()
 
     def gate_block(b, _):
         r = block(b, RB)
         n = normed[r, :]
-        q[r, :] = nn(n, wall[:, 0:W])
+        qq = nn(n, wall[:, 0:W])
+        q_sig[r, :] = jax.nn.sigmoid(qq)
+        qh[r, :], ql[r, :] = split(qq * (0.125 * LOG2E))
         gg = nn(n, wall[:, 3 * W : 4 * W])
         g[r, :] = gg
         dm = dmix[r, :] + nt(co[r, :], woo[...])
@@ -347,34 +397,47 @@
     def joined(a):
         return jnp.where(lane_half, a[0:NODES], a[NODES : 2 * NODES])
 
-    def forward_block(s, _):
-        r = block(s, NODES)
-        listed = adjacent[:, r]
-        count = jnp.zeros((NODES, NODES), F32)
-        for j in range(listed.shape[0]):
-            count = count + jnp.where(listed[j : j + 1, :] == node_of, 1.0, 0.0)
-        weight = jnp.where(count > 0.0, jnp.log(jnp.maximum(count, 1.0)) * LOG2E, -1e30)
-        weight = lanes_cat(weight, weight)
-        for p in range(PAIRS):
-            ls = slice(p * 128, (p + 1) * 128)
-            qh, ql = split(q[r, ls] * (0.125 * LOG2E))
-            kh, kl = split(k[r, ls])
-            vh, vl = split(v[r, ls])
-            qbh = apart(qh)
-            score = nt(lanes_cat(kh, kl, kh), lanes_cat(qbh, qbh, apart(ql))) + weight
+    FU = 4
+    lanes = [slice(p * 128, (p + 1) * 128) for p in range(PAIRS)]
+
+    def forward_block(i, _):
+        chains = [(i * FU + u, p) for u in range(FU) for p in range(PAIRS)]
+        weights = []
+        for u in range(FU):
+            listed = adjacent[:, block(i * FU + u, NODES)]
+            count = jnp.zeros((NODES, NODES), F32)
+            for j in range(listed.shape[0]):
+                count = count + jnp.where(listed[j : j + 1, :] == node_of, 1.0, 0.0)
+            weight = jnp.where(count > 0.0, jnp.log(jnp.maximum(count, 1.0)) * LOG2E, -1e30)
+            weights.append(lanes_cat(weight, weight))
+        scores = []
+        for s, p in chains:
+            r, ls = block(s, NODES), lanes[p]
+            high, low = kh[r, ls], kl[r, ls]
+            qbh = apart(qh[r, ls])
+            scores.append(
+                nt(lanes_cat(high, low, high), lanes_cat(qbh, qbh, apart(ql[r, ls])))
+            )
+        probs = []
+        for j, score in enumerate(scores):
+            score = score + weights[j // PAIRS]
             e = jnp.exp2(score - jnp.max(score, axis=0, keepdims=True))
-            pr = e * (1.0 / jnp.sum(e, axis=0, keepdims=True))
-            ph, plow = split(pr)
-            prob[s, p, 0] = ph
-            prob[s, p, 1] = plow
+            probs.append(split(e * (1.0 / jnp.sum(e, axis=0, keepdims=True))))
+        for (s, p), (high, low) in zip(chains, probs):
+            prob[s, p, 0] = high
+            prob[s, p, 1] = low
+        for (s, p), (high, low) in zip(chains, probs):
+            r, ls = block(s, NODES), lanes[p]
+            vhigh = vh[r, ls]
             o = tn(
-                rows_cat(ph, plow),
-                rows_cat(lanes_cat(vh, vl), lanes_cat(vh, jnp.zeros_like(vh))),
+                rows_cat(high, low),
+                rows_cat(lanes_cat(vhigh, vl[r, ls]), lanes_cat(vhigh, jnp.zeros_like(vhigh))),
             )
             att[r, ls] = joined(o[:, 0:128] + o[:, 128:256])
         return 0
 
-    lax.fori_loop(0, NB, forward_block, 0)
+    adjacent_load.wait()
+    lax.fori_loop(0, NB // FU, forward_block, 0)
 
     mats, totals = ar_result(0, ar0)
     square = (2, 128, 128)
@@ -390,14 +453,16 @@
         den_w.append(rows_cat(th, tl))
         back_w.append(lanes_cat(sh, sh, sl))
 
-    def glob_block(s, carry):
-        r = block(s, NODES)
-        keep = (1 - period[s]).astype(F32)
+    GU = 4
+
+    def glob_block(i, carry):
+        r = block(i, GU * NODES)
+        keep = [(1 - period[i * GU + u]).astype(F32) for u in range(GU)]
         sums, tots = carry
         new_sums, new_tots = [], []
         for p in range(PAIRS):
-            ls = slice(p * 128, (p + 1) * 128)
-            qp = jax.nn.sigmoid(q[r, ls])
+            ls = lanes[p]
+            qp = q_sig[r, ls]
             qpb = qp.astype(BF)
             num = nn(qpb, num_w[p])
             den = nt(qpb, den_w[p])
@@ -406,7 +471,8 @@
             at = att[r, ls] + glob
             mix[r, ls] = ((1.0 - BETA) * g[r, ls] * at + BETA * at).astype(BF)
             low4[GATE, r, ls] = (dmix[r, ls] * (1.0 - BETA) * at).astype(BF)
-            dnum = (keep * datt[r, ls]) * inv
+            da = datt[r, ls]
+            dnum = rows_cat(*[keep[u] * da[u * NODES : (u + 1) * NODES] for u in range(GU)]) * inv
             dh, dl = split(dnum)
             th, tl = split(dnum * glob)
             dden = -nn(lanes_cat(th, tl), rows_cat(ones_bd, ones_bd))
@@ -416,7 +482,7 @@
             new_tots.append(tots[p] + jnp.sum(dden * qp, axis=0, keepdims=True))
         return tuple(new_sums), tuple(new_tots)
 
-    carry = lax.fori_loop(0, NB, glob_block, zero_sums())
+    carry = lax.fori_loop(0, NB // GU, glob_block, zero_sums())
     pack_sums(1, carry)
     ar1 = ar_scatter(1)
     mix_copy = send(mix, mixo, mix_sems, (0,), partner)
@@ -507,9 +573,10 @@
             for i, (_, dv_) in enumerate(a_peers)
         ]
 
-    def w_end(copies):
+    def w_keep(w, copies):
         for cp in copies:
             cp.wait()
+        store(fin.at[w], fin_hbm.at[w])
 
     weight_grads((GATE,))
     gate_copies = w_scatter(GATE)
@@ -517,66 +584,72 @@
     out_grads()
     out_copies = w_scatter(OUT)
 
-    def backward_block(s, _):
-        r = block(s, NODES)
-        for p in range(PAIRS):
-            ls = slice(p * 128, (p + 1) * 128)
-            qh, ql = split(q[r, ls])
-            kh, kl = split(k[r, ls])
-            vh, vl = split(v[r, ls])
+    BU = 4
+
+    def backward_block(i, _):
+        chains = [(block(i * BU + u, NODES), i * BU + u, p) for u in range(BU) for p in range(PAIRS)]
+        outs, dps = [], []
+        for r, s, p in chains:
+            ls = lanes[p]
             oh, ol = split(datt[r, ls])
-            qbh, qbl = apart(qh), apart(ql)
-            obh, obl = apart(oh), apart(ol)
-            ph = prob[s, p, 0]
-            plow = prob[s, p, 1]
-            pr = ph.astype(F32) + plow.astype(F32)
-            dp = nt(lanes_cat(vh, vl, vh), lanes_cat(obh, obh, obl))
-            ds = pr * (dp - jnp.sum(pr * dp, axis=0, keepdims=True)) * 0.125
-            dsh, dsl = split(ds)
-            got = nn(ph, lanes_cat(obh, obl))
-            dv[r, ls] = got[:, 0:128] + got[:, 128:256] + nn(plow, obh)
-            got = nn(dsh, lanes_cat(qbh, qbl))
-            dk[r, ls] = got[:, 0:128] + got[:, 128:256] + nn(dsl, qbh)
+            oh, ol = apart(oh), apart(ol)
+            outs.append((oh, ol))
+            high = vh[r, ls]
+            dps.append(nt(lanes_cat(high, vl[r, ls], high), lanes_cat(oh, oh, ol)))
+        dss = []
+        for (r, s, p), dp in zip(chains, dps):
+            pr = prob[s, p, 0].astype(F32) + prob[s, p, 1].astype(F32)
+            dss.append(split(pr * (dp - jnp.sum(pr * dp, axis=0, keepdims=True))))
+        for (r, s, p), (oh, ol) in zip(chains, outs):
+            got = nn(prob[s, p, 0], lanes_cat(oh, ol))
+            dv[r, lanes[p]] = got[:, 0:128] + got[:, 128:256] + nn(prob[s, p, 1], oh)
+        for (r, s, p), (high, low) in zip(chains, dss):
+            ls = lanes[p]
+            qbh = apart(qh[r, ls])
+            got = nn(high, lanes_cat(qbh, apart(ql[r, ls])))
+            dk[r, ls] = (got[:, 0:128] + got[:, 128:256] + nn(low, qbh)) * (1.0 / LOG2E)
+        for (r, s, p), (high, low) in zip(chains, dss):
+            ls = lanes[p]
+            khigh = kh[r, ls]
             got = tn(
-                rows_cat(dsh, dsl),
-                rows_cat(lanes_cat(kh, kl), lanes_cat(kh, jnp.zeros_like(kh))),
+                rows_cat(high, low),
+                rows_cat(lanes_cat(khigh, kl[r, ls]), lanes_cat(khigh, jnp.zeros_like(khigh))),
             )
-            low4[QUERY, r, ls] = (dq[r, ls] + joined(got[:, 0:128] + got[:, 128:256])).astype(BF)
+            got = joined(got[:, 0:128] + got[:, 128:256]) * 0.125
+            low4[QUERY, r, ls] = (dq[r, ls] + got).astype(BF)
         return 0
 
-    FIRST = NB // 2
+    FIRST = NB // BU // 2
     lax.fori_loop(0, FIRST, backward_block, 0)
     ar1 = ar_reduce(1, ar1)
+    lax.fori_loop(FIRST, NB // BU, backward_block, 0)
     gate_copies = w_middle(GATE, gate_copies)
     out_copies = w_middle(OUT, out_copies)
-    lax.fori_loop(FIRST, NB, backward_block, 0)
-    gate_copies = w_spread(GATE, gate_copies)
-    out_copies = w_spread(OUT, out_copies)
     weight_grads((QUERY,))
     query_copies = w_scatter(QUERY)
-    gate_copies = w_gather(GATE, gate_copies)
-    out_copies = w_gather(OUT, out_copies)
 
     mats, totals = ar_result(1, ar1)
     dsum = [m.astype(BF) for m in mats]
 
-    def key_block(s, _):
-        r = block(s, NODES)
-        mask = live_mask(s)
+    KU = 4
+
+    def key_block(i, _):
+        r = block(i, KU * NODES)
         for p in range(PAIRS):
-            ls = slice(p * 128, (p + 1) * 128)
-            sig = jax.nn.sigmoid(k[r, ls])
-            kp = jnp.where(mask, sig, 0.0)
-            dkp = nt(v[r, ls].astype(BF), dsum[p]) + totals[p]
+            ls = lanes[p]
+            sig = k_sig[r, ls]
+            kp = live_rows(i * KU, sig, KU)
+            dkp = nt(vh[r, ls], dsum[p]) + totals[p]
             low4[KEY, r, ls] = (dk[r, ls] + dkp * kp * (1.0 - sig)).astype(BF)
             low4[VALUE, r, ls] = (dv[r, ls] + nn(kp.astype(BF), dsum[p])).astype(BF)
         return 0
 
-    lax.fori_loop(0, NB, key_block, 0)
+    lax.fori_loop(0, NB // KU, key_block, 0)
     weight_grads((KEY, VALUE))
     key_copies = w_scatter(KEY)
     value_copies = w_scatter(VALUE)
-    query_copies = w_middle(QUERY, query_copies)
+    gate_copies = w_spread(GATE, gate_copies)
+    out_copies = w_spread(OUT, out_copies)
 
     def normed_block(b, _):
         r = block(b, RB)
@@ -606,20 +679,25 @@
                 send(st_send.at[piece], st_recv.at[piece], dn_sems, (1, i), partner),
             )
         )
-    query_copies = w_spread(QUERY, query_copies)
+        if i == 1:
+            query_copies = w_middle(QUERY, query_copies)
     key_copies = w_middle(KEY, key_copies)
     value_copies = w_middle(VALUE, value_copies)
+    query_copies = w_spread(QUERY, query_copies)
+    gate_copies = w_gather(GATE, gate_copies)
+    out_copies = w_gather(OUT, out_copies)
 
     def out_block(b, _):
         r = block(b, RB)
         got = nn(mix[r, :], wo[own_rows, :]) + nn(mixo[r, :], wo[oth_rows, :])
-        layer_out[r, :] = (x[r, :].astype(F32) + got).astype(BF)
+        mixo[r, :] = (x[r, :].astype(F32) + got).astype(BF)
         return 0
 
     lax.fori_loop(0, NR, out_block, 0)
-    query_copies = w_gather(QUERY, query_copies)
+    store(mixo, layer_out)
     key_copies = w_spread(KEY, key_copies)
     value_copies = w_spread(VALUE, value_copies)
+    query_copies = w_gather(QUERY, query_copies)
 
     def input_block(b, carry):
         gain_sum, bias_sum = carry
@@ -632,7 +710,7 @@
         s2 = st[:, 64:65] * (1.0 / (2 * W))
         ha = (x[r, :].astype(F32) - mean) * rstd
         inner = rstd * (dn * gain_own - s1 - ha * s2)
-        input_grad[r, :] = (c[r, :].astype(F32) + inner).astype(BF)
+        co[r, :] = (c[r, :].astype(F32) + inner).astype(BF)
         return (
             gain_sum + jnp.sum(dn * ha, axis=0, keepdims=True),
             bias_sum + jnp.sum(dn, axis=0, keepdims=True),
@@ -643,6 +721,8 @@
         for cp in dn_copies[i]:
             cp.wait_recv()
         carry = lax.fori_loop(i * (NR // DC), (i + 1) * (NR // DC), input_block, carry)
+        piece = pl.ds(i * (R // DC), R // DC)
+        store(co.at[piece], input_grad.at[piece])
 
     row = lax.broadcasted_iota(jnp.int32, (8, W), 0)
     terms = jnp.where(row == 0, carry[0], jnp.where(row == 1, carry[1], 0.0))
@@ -667,9 +747,15 @@
         total = gb_hi[0]
         for i in range(1, C):
             total = total + gb_hi[i]
-    small_grad[...] = total
-    for copies in (gate_copies, out_copies, query_copies, key_copies, value_copies):
-        w_end(copies)
+    gain_grad[...] = total[0:1].reshape(W)
+    bias_grad[...] = total[1:2].reshape(W)
+    w_keep(GATE, gate_copies)
+    w_keep(OUT, out_copies)
+    w_keep(QUERY, query_copies)
+    w_keep(KEY, key_copies)
+    w_keep(VALUE, value_copies)
+    for cp in stores:
+        cp.wait()
     for cp in core_copies:
         cp.wait_send()
     mix_copy.wait_send()
@@ -706,20 +792,27 @@
     dma = pltpu.SemaphoreType.DMA
     vmem = pl.BlockSpec(memory_space=pltpu.VMEM)
     smem = pl.BlockSpec(memory_space=pltpu.SMEM)
-    layer_output, input_grad, small, fin = pl.pallas_call(
+    hbm = pl.BlockSpec(memory_space=pl.ANY)
+    layer_output, input_grad, gain_grad, bias_grad, fin = pl.pallas_call(
         functools.partial(layer_kernel, groups),
         name="layer_kernel",
         out_shape=(
             jax.ShapeDtypeStruct((R, W), BF),
             jax.ShapeDtypeStruct((R, W), BF),
-            jax.ShapeDtypeStruct((8, W), F32),
+            jax.ShapeDtypeStruct((W,), F32),
+            jax.ShapeDtypeStruct((W,), F32),
             jax.ShapeDtypeStruct((5, D, W), BF),
         ),
-        in_specs=[vmem] * 10 + [smem] * 2,
-        out_specs=(vmem, vmem, vmem, vmem),
+        in_specs=[hbm] * 2 + [vmem] * 2 + [hbm] * 6 + [smem] * 2,
+        out_specs=(hbm, hbm, vmem, vmem, hbm),
         scratch_shapes=[
             VM((R, W), BF),
             VM((R, W), BF),
+            VM((R, W), BF),
+            VM((R, W), BF),
+            VM((D, W), BF),
+            VM((adjacent_vertices.shape[1], R), jnp.int32),
+            VM((5, D, W), BF),
             VM((16, W), F32),
             VM((16, W), F32),
             VM((W, W), BF),
@@ -729,20 +822,21 @@
             VM((R, 128), F32),
             VM((R, W), F32),
             VM((R, W), F32),
-            VM((R, W), F32),
+            VM((R, W), BF),
+            VM((R, W), BF),
+            VM((R, W), BF),
+            VM((R, W), BF),
+            VM((R, W), BF),
+            VM((R, W), BF),
             VM((R, W), F32),
             VM((R, W), F32),
             VM((R, W), F32),
             VM((R, W), F32),
             VM((NB, PAIRS, 2, NODES, 2 * NODES), BF),
             VM((R, W), F32),
-            VM((R, W), F32),
-            VM((R, W), F32),
             VM((4, R, W), BF),
             VM((R, W), BF),
             VM((R, W), BF),
-            VM((R, W), F32),
-            VM((R, W), F32),
             VM((R, W), F32),
             VM((R, 128), F32),
             VM((R, 128), F32),
@@ -760,6 +854,8 @@
             VM((8, W), F32),
             VM((L, 8, W), F32),
             VM((C, 8, W), F32),
+            dma((15,)),
+            dma((10,)),
             dma((2, 8)),
             dma((2, 1)),
             dma((2, 2, 4)),
@@ -776,8 +872,8 @@
     )(
         node_input,
         cotangent,
-        norm_gain.reshape(1, W),
-        norm_bias.reshape(1, W),
+        norm_gain,
+        norm_bias,
         query_weight,
         key_weight,
         value_weight,
@@ -787,18 +883,48 @@
         active_vertex_tally,
         training_period,
     )
-    full = fin.astype(F32)
-    return (
-        layer_output,
-        input_grad,
-        small[0],
-        small[1],
-        full[QUERY],
-        full[KEY],
-        full[VALUE],
-        full[GATE],
-        full[OUT],
-    )
+    return pl.pallas_call(
+        finish_kernel,
+        name="finish_kernel",
+        out_shape=(
+            jax.ShapeDtypeStruct((R, W), BF),
+            jax.ShapeDtypeStruct((R, W), BF),
+            jax.ShapeDtypeStruct((W,), F32),
+            jax.ShapeDtypeStruct((W,), F32),
+        )
+        + tuple(jax.ShapeDtypeStruct((D, W), F32) for _ in range(5)),
+        in_specs=[hbm, hbm, vmem, vmem, hbm],
+        out_specs=(hbm, hbm, vmem, vmem) + (hbm,) * 5,
+        scratch_shapes=[VM((5, D, W), BF), VM((5, D, W), F32), VM((2, R, W), BF), dma((14,))],
+    )(layer_output, input_grad, gain_grad, bias_grad, fin)
+
+
+def finish_kernel(
+    lo_in, ig_in, gain_in, bias_in, fin, lo, ig, gain, bias, gq, gk, gv, gg, go, low, full, wide, sems
+):
+    loads = []
+
+    def begin(src, dst, into):
+        copy = pltpu.make_async_copy(src, dst, sems.at[len(into) + (0 if into is loads else 7)])
+        copy.start()
+        into.append(copy)
+
+    for i in range(5):
+        begin(fin.at[i], low.at[i], loads)
+    begin(lo_in, wide.at[0], loads)
+    begin(ig_in, wide.at[1], loads)
+    gain[...] = gain_in[...]
+    bias[...] = bias_in[...]
+    stores = []
+    for i, out in enumerate((gq, gk, gv, gg, go)):
+        loads[i].wait()
+        full[i] = low[i].astype(F32)
+        begin(full.at[i], out, stores)
+    for i, out in enumerate((lo, ig)):
+        loads[5 + i].wait()
+        begin(wide.at[i], out, stores)
+    for cp in stores:
+        cp.wait()
 
 
 def factors(count):

time: 114 us -> 83.9 us (0.74)
  Pallas kernels: 104 us -> 82.9 us
  local copies, waits for them, and re-layouts: 7.55 us -> 0 us
  other arithmetic: 1.55 us -> 0 us
    pallas_call x1, Pallas kernels: 104 us -> 78.4 us  [shards(): pl.pallas_call(functools.partial(layer_kernel, groups), name='layer_kerne...]
    pallas_call x0 -> x1, Pallas kernels: none -> 4.54 us  [shards(): pl.pallas_call(finish_kernel, name='finish_kernel', out_shape=(jax.ShapeD...]
    reshape x2 -> x0, local copies, waits for them, and re-layouts: 2.44 us -> none  [the longest x1 1.22 us: shards(): norm_gain.reshape(1, W)]
    unnamed x6 -> x0, local copies, waits for them, and re-layouts: 2.25 us -> none
    convert_element_type x1 -> x0, other arithmetic: 1.55 us -> none  [shards(): full = fin.astype(F32)]
    squeeze x1 -> x0, local copies, waits for them, and re-layouts: 1.52 us -> none  [shards(): full[OUT]]
    slice x1 -> x0, local copies, waits for them, and re-layouts: 1.34 us -> none  [shards(): small[1]]
where the time goes in v2:
time: 83.9 us; the launch traced here: 83.8 us
  Pallas kernels  82.9 us (99%)
    pallas_call x1, Pallas kernels, shards(): pl.pallas_call(functools.partial(layer_kernel, groups), name='layer_kerne...  78.4 us
    pallas_call x1, Pallas kernels, shards(): pl.pallas_call(finish_kernel, name='finish_kernel', out_shape=(jax.ShapeD...  4.54 us

profile of v2, /device:TPU:0, one launch (start us, length us, event | category | flops | bytes accessed | tf_op | source)
XLA Modules:
  0.0 83.8 jit_solution(1257237338671228628)
XLA Ops:
  0.6 78.4 %layer_kernel.1 = (bf16[2048,256]{1,0:T(8,128)(2,1)}, bf16[2048,256]{1,0:T(8,128)(2,1)}, f32[256]{0:T(256)}, f32[256]{0:T(256)}, bf16[5,512,256]{2,1,0:T(8,128)(2,1)}) custom-call(bf16[2048,256]{1,0:T(8,128)(2,1)} %x_hbm.1, bf16[2048,256]{1,0:T(8,128)(2,1)} %c_hbm.1, bf16[256]{0:T(256)(128)(2,1)} %gain.1, bf16[256]{0:T(256)(128)(2,1)} %bias.1, ...), custom_call_target="tpu_custom_call" | custom-call | tf_op jit(solution)/shard_map/layer_kernel/pallas_call | solution.py:796
  79.1 4.5 %finish_kernel.1 = (bf16[2048,256]{1,0:T(8,128)(2,1)}, bf16[2048,256]{1,0:T(8,128)(2,1)}, f32[256]{0:T(256)}, f32[256]{0:T(256)}, f32[512,256]{1,0:T(8,128)}, /*...) custom-call(bf16[2048,256]{1,0:T(8,128)(2,1)} %get-tuple-element.14.lo_in, ...), custom_call_target="tpu_custom_call" | custom-call | tf_op jit(solution)/shard_map/finish_kernel/pallas_call | solution.py:886

commit v3 on v2

--- a/solution.py
+++ b/solution.py
@@ -14,7 +14,6 @@
 F32 = jnp.float32
 MESH = pl.DeviceIdType.MESH
 NODES = 128
-CHUNKS = 16
 QUERY, KEY, VALUE, GATE, OUT = 0, 1, 2, 3, 4
 
 
@@ -102,7 +101,8 @@
     st_recv,
     sum_part,
     sum_recv,
-    sum_red,
+    sum_mid,
+    sum_z,
     sum_hi,
     sum_full,
     part,
@@ -113,6 +113,7 @@
     hrecv,
     gb_part,
     gb_recv,
+    gb_z,
     gb_hi,
     load_sems,
     store_sems,
@@ -124,7 +125,6 @@
     w_sems,
     wh_sems,
     gb_sems,
-    gbh_sems,
 ):
     A, B, C = groups
     L = A * B
@@ -142,30 +142,34 @@
     def dev(h_, b_, a_):
         return (h_ * L + b_ * A + a_, head)
 
-    lo_peers = [(hi * L + lax.rem(lo + d, L), head) for d in range(1, L)]
-    hi_peers = [(lax.rem(hi + d, C) * L + lo, head) for d in range(1, C)]
     a_peers = [(lax.rem(al + d, A), dev(hi, bl, lax.rem(al + d, A))) for d in range(1, A)]
     b_peers = [(lax.rem(bl + d, B), dev(hi, lax.rem(bl + d, B), al)) for d in range(1, B)]
+    h_peers = [(lax.rem(hi + d, C), dev(lax.rem(hi + d, C), bl, al)) for d in range(1, C)]
     partner = (me, other)
     own_rows = block(head, W)
     oth_rows = block(other, W)
 
-    def send(src, dst, sems, index, to):
-        copy = pltpu.make_async_remote_copy(
+    def send(src, dst, send_sem, recv_sem, to):
+        pltpu.make_async_remote_copy(
             src_ref=src,
             dst_ref=dst,
-            send_sem=sems.at[(0,) + index],
-            recv_sem=sems.at[(1,) + index],
+            send_sem=send_sem,
+            recv_sem=recv_sem,
             device_id=to,
             device_id_type=MESH,
-        )
-        copy.start()
-        return copy
+        ).start()
+
+    def bytes_of(ref, sem):
+        pltpu.make_async_copy(ref, ref, sem).wait()
+
+    def wait_both(ref, sems, index):
+        bytes_of(ref, sems.at[(0,) + index])
+        bytes_of(ref, sems.at[(1,) + index])
 
     dk, dv, dn_own, dn_send = att, q_sig, g, dmix
 
     barrier = pltpu.get_barrier_semaphore()
-    greeted = [partner] + lo_peers + hi_peers
+    greeted = [partner] + [to for _, to in a_peers + b_peers + h_peers]
     for to in greeted:
         pl.semaphore_signal(barrier, inc=1, device_id=to, device_id_type=MESH)
 
@@ -202,18 +206,15 @@
     gbs[8:16, :] = jnp.broadcast_to(bias[...].astype(F32).reshape(1, W), (8, W))
     pl.semaphore_wait(barrier, len(greeted))
 
-    CC = 2
-    core_copies = [send(gbs, gbo, core_sems, (0,), partner)]
-    for i in range(XC):
-        piece = pl.ds(i * (R // XC), R // XC)
+    send(gbs, gbo, core_sems.at[0, 0], core_sems.at[1, 0], partner)
+    pieces = [pl.ds(i * (R // XC), R // XC) for i in range(XC)]
+    for i, piece in enumerate(pieces):
         x_loads[i].wait()
-        core_copies.append(send(x.at[piece], xo.at[piece], core_sems, (1 + i,), partner))
+        send(x.at[piece], xo.at[piece], core_sems.at[0, 3], core_sems.at[1, 3 + i], partner)
     wo_load.wait()
-    core_copies.append(send(wo.at[oth_rows], woo, core_sems, (1 + XC,), partner))
+    send(wo.at[oth_rows], woo, core_sems.at[0, 1], core_sems.at[1, 1], partner)
     c_load.wait()
-    for i in range(CC):
-        piece = pl.ds(i * (R // CC), R // CC)
-        core_copies.append(send(c.at[piece], co.at[piece], core_sems, (2 + XC + i,), partner))
+    send(c, co, core_sems.at[0, 2], core_sems.at[1, 2], partner)
 
     RB = 256
     NR = R // RB
@@ -226,7 +227,7 @@
     lax.fori_loop(0, NR, own_dmix, 0)
 
     sum_part[...] = jnp.zeros_like(sum_part)
-    core_copies[0].wait_recv()
+    bytes_of(gbo, core_sems.at[1, 0])
     gain_own, bias_own = gbs[0:1, :], gbs[8:9, :]
     gain_oth, bias_oth = gbo[0:1, :], gbo[8:9, :]
     lane_half = lax.broadcasted_iota(jnp.int32, (1, 128), 1) < 64
@@ -242,6 +243,11 @@
         )
 
     def norm_block(b, carry):
+        @pl.when(lax.rem(b, NR // XC) == 0)
+        def _():
+            i = b // (NR // XC)
+            bytes_of(xo.at[block(i, R // XC)], core_sems.at[1, 3 + i])
+
         r = block(b, RB)
         xa = x[r, :].astype(F32)
         xb = xo[r, :].astype(F32)
@@ -287,89 +293,90 @@
 
     for cp in w_loads[0:4]:
         cp.wait()
-    carry = zero_sums()
-    for i in range(XC):
-        core_copies[1 + i].wait_recv()
-        carry = lax.fori_loop(i * (NR // XC), (i + 1) * (NR // XC), norm_block, carry)
+    carry = lax.fori_loop(0, NR, norm_block, zero_sums())
 
     def pack_sums(slot, carry):
         sums, totals = carry
+        packed = rows_cat(
+            *[jnp.where(lane_half, sums[p][0:64], sums[p][64:128]) for p in range(PAIRS)]
+        )
+        for j in range(A):
+            sum_part[slot, j, 0:SR, :] = packed[j * SR : (j + 1) * SR]
+            for p in range(PAIRS):
+                sum_part[slot, j, SR + p : SR + p + 1, :] = totals[p]
+
+    SR = 64 * PAIRS // A
+
+    def ar_scatter(slot):
+        for i, (j, to) in enumerate(a_peers):
+            send(
+                sum_part.at[slot, j],
+                sum_recv.at[slot, i],
+                ar_sems.at[0, slot, 0],
+                ar_sems.at[1, slot, 0],
+                to,
+            )
+
+    def ar_middle(slot):
+        wait_both(sum_recv.at[slot], ar_sems, (slot, 0))
+        total = sum_part[slot, al]
+        for i in range(A - 1):
+            total = total + sum_recv[slot, i]
+        sum_mid[slot] = total
+        for i, (_, to) in enumerate(b_peers):
+            send(
+                sum_mid.at[slot],
+                sum_z.at[slot, i],
+                ar_sems.at[0, slot, 1],
+                ar_sems.at[1, slot, 1],
+                to,
+            )
+
+    def ar_gather(slot):
+        wait_both(sum_z.at[slot], ar_sems, (slot, 1))
+        total = sum_mid[slot]
+        for i in range(B - 1):
+            total = total + sum_z[slot, i]
+        if C > 1:
+            sum_mid[slot] = total
+            for i, (_, to) in enumerate(h_peers):
+                send(
+                    sum_mid.at[slot],
+                    sum_hi.at[slot, i],
+                    arh_sems.at[0, slot],
+                    arh_sems.at[1, slot],
+                    to,
+                )
+            wait_both(sum_hi.at[slot], arh_sems, (slot,))
+            for i in range(C - 1):
+                total = total + sum_hi[slot, i]
+        sum_full[slot, al] = total
+        for i, (_, to) in enumerate(a_peers):
+            send(
+                sum_full.at[slot, al],
+                sum_full.at[slot, al],
+                ar_sems.at[0, slot, 2],
+                ar_sems.at[1, slot, 2],
+                to,
+            )
+
+    def ar_result(slot):
+        wait_both(sum_recv.at[slot], ar_sems, (slot, 2))
+        mats, totals = [], []
+        packed = rows_cat(*[sum_full[slot, j, 0:SR, :] for j in range(A)])
         for p in range(PAIRS):
-            packed = jnp.where(lane_half, sums[p][0:64], sums[p][64:128])
-            for j in range(8):
-                sum_part[slot, p * 8 + j, 0:8, :] = packed[j * 8 : (j + 1) * 8]
-            for j in range(CHUNKS):
-                sum_part[slot, j, 8 + p : 9 + p, :] = totals[p]
-
-    PER = CHUNKS // L
-
-    def ar_scatter(slot):
-        mine = block(lo, PER)
-        sum_recv[slot, pl.ds(lo, 1)] = sum_part[slot, mine].reshape((1,) + sum_part.shape[1:][:0] + (PER,) + sum_part.shape[2:])
-        copies = []
-        for d in range(1, L):
-            to = lax.rem(lo + d, L)
-            copies.append(
-                send(
-                    sum_part.at[slot, block(to, PER)],
-                    sum_recv.at[slot, lo],
-                    ar_sems,
-                    (slot, 0, d - 1),
-                    lo_peers[d - 1],
-                )
-            )
-        return copies
-
-    def ar_reduce(slot, copies):
-        for cp in copies:
-            cp.wait()
-        total = sum_recv[slot, 0]
-        for i in range(1, L):
-            total = total + sum_recv[slot, i]
-        if C > 1:
-            sum_hi[slot, pl.ds(hi, 1)] = total[None]
-            sum_red[slot] = total
-            hc = [
-                send(sum_red.at[slot], sum_hi.at[slot, hi], arh_sems, (slot, d - 1), hi_peers[d - 1])
-                for d in range(1, C)
-            ]
-            for cp in hc:
-                cp.wait()
-            total = sum_hi[slot, 0]
-            for i in range(1, C):
-                total = total + sum_hi[slot, i]
-        sum_red[slot] = total
-        sum_full[slot, block(lo, PER)] = total[:, 0:8, :]
-        return [
-            send(
-                sum_red.at[slot, :, pl.ds(0, 8)],
-                sum_full.at[slot, block(lo, PER)],
-                ar_sems,
-                (slot, 1, d - 1),
-                lo_peers[d - 1],
-            )
-            for d in range(1, L)
-        ]
-
-    def ar_result(slot, copies):
-        for cp in copies:
-            cp.wait()
-        mats, totals = [], []
-        for p in range(PAIRS):
-            packed = rows_cat(*[sum_full[slot, p * 8 + j] for j in range(8)])
-            mats.append(
-                rows_cat(jnp.where(lane_half, packed, 0.0), jnp.where(lane_half, 0.0, packed))
-            )
-            totals.append(sum_red[slot, 0, 8 + p : 9 + p, :])
+            own = packed[p * 64 : (p + 1) * 64]
+            mats.append(rows_cat(jnp.where(lane_half, own, 0.0), jnp.where(lane_half, 0.0, own)))
+            totals.append(sum_full[slot, 0, SR + p : SR + p + 1, :])
         return mats, totals
 
     pack_sums(0, carry)
-    ar0 = ar_scatter(0)
+    ar_scatter(0)
 
     for cp in w_loads[4:]:
         cp.wait()
-    for cp in core_copies[1 + XC :]:
-        cp.wait_recv()
+    bytes_of(woo, core_sems.at[1, 1])
+    bytes_of(co, core_sems.at[1, 2])
 
     def gate_block(b, _):
         r = block(b, RB)
@@ -385,7 +392,7 @@
         return 0
 
     lax.fori_loop(0, NR, gate_block, 0)
-    ar0 = ar_reduce(0, ar0)
+    ar_middle(0)
 
     half_row = jnp.where(lane_half, 1.0, 0.0)
     half_a = jnp.broadcast_to(half_row, (NODES, 128)).astype(BF)
@@ -401,6 +408,10 @@
     lanes = [slice(p * 128, (p + 1) * 128) for p in range(PAIRS)]
 
     def forward_block(i, _):
+        @pl.when(i == NB // FU // 2)
+        def _():
+            ar_gather(0)
+
         chains = [(i * FU + u, p) for u in range(FU) for p in range(PAIRS)]
         weights = []
         for u in range(FU):
@@ -439,7 +450,7 @@
     adjacent_load.wait()
     lax.fori_loop(0, NB // FU, forward_block, 0)
 
-    mats, totals = ar_result(0, ar0)
+    mats, totals = ar_result(0)
     square = (2, 128, 128)
     same_head = (lax.broadcasted_iota(jnp.int32, (128, 128), 0) < 64) == (
         lax.broadcasted_iota(jnp.int32, (128, 128), 1) < 64
@@ -484,8 +495,8 @@
 
     carry = lax.fori_loop(0, NB // GU, glob_block, zero_sums())
     pack_sums(1, carry)
-    ar1 = ar_scatter(1)
-    mix_copy = send(mix, mixo, mix_sems, (0,), partner)
+    ar_scatter(1)
+    send(mix, mixo, mix_sems.at[0], mix_sems.at[1], partner)
 
     KB = 512
 
@@ -518,75 +529,105 @@
     PA = D // A
     PB = PA // B
 
+    QUERIES, KEYVALUE, GATEOUT = 0, 1, 2
+    span = {QUERIES: pl.ds(0, 1), KEYVALUE: pl.ds(1, 2), GATEOUT: pl.ds(3, 2)}
+    kinds_of = {QUERIES: (QUERY,), KEYVALUE: (KEY, VALUE), GATEOUT: (GATE, OUT)}
+
     def w_scatter(w):
-        psend[w] = part[w].astype(BF)
-        return [
-            send(psend.at[w, block(to, PA)], precv.at[w, i], w_sems, (w, 0, i), dv_)
-            for i, (to, dv_) in enumerate(a_peers)
-        ]
-
-    def w_middle(w, copies):
-        for cp in copies:
-            cp.wait()
-        total = part[w, block(al, PA), :]
-        for i in range(A - 1):
-            total = total + precv[w, i].astype(F32)
-        zpart[w] = total
-        return [
-            send(zpart.at[w, block(to, PB)], zrecv.at[w, i], w_sems, (w, 1, i), dv_)
-            for i, (to, dv_) in enumerate(b_peers)
-        ]
-
-    def w_spread(w, copies):
-        for cp in copies:
-            cp.wait()
-        total = zpart[w, block(bl, PB), :]
-        for i in range(B - 1):
-            total = total + zrecv[w, i]
-        here = pl.ds(pl.multiple_of(al * PA + bl * PB, PB), PB)
+        for kind in kinds_of[w]:
+            psend[kind] = part[kind].astype(BF)
+        for i, (j, to) in enumerate(a_peers):
+            send(
+                psend.at[span[w], block(j, PA)],
+                precv.at[i, span[w]],
+                w_sems.at[0, w, 0],
+                w_sems.at[1, w, 0],
+                to,
+            )
+
+    def w_middle(w):
+        wait_both(precv.at[:, span[w]], w_sems, (w, 0))
+        for kind in kinds_of[w]:
+            total = part[kind, block(al, PA), :]
+            for i in range(A - 1):
+                total = total + precv[i, kind].astype(F32)
+            zpart[kind] = total
+        for i, (j, to) in enumerate(b_peers):
+            send(
+                zpart.at[span[w], block(j, PB)],
+                zrecv.at[i, span[w]],
+                w_sems.at[0, w, 1],
+                w_sems.at[1, w, 1],
+                to,
+            )
+
+    here = pl.ds(pl.multiple_of(al * PA + bl * PB, PB), PB)
+
+    def w_spread(w):
+        wait_both(zrecv.at[:, span[w]], w_sems, (w, 1))
+        totals = {}
+        for kind in kinds_of[w]:
+            total = zpart[kind, block(bl, PB), :]
+            for i in range(B - 1):
+                total = total + zrecv[i, kind]
+            totals[kind] = total
         if C > 1:
-            hrecv[w, pl.ds(hi, 1)] = total[None]
-            zpart[w, block(bl, PB), :] = total
-            hc = [
+            for kind in kinds_of[w]:
+                zpart[kind, block(bl, PB), :] = totals[kind]
+            for i, (_, to) in enumerate(h_peers):
                 send(
-                    zpart.at[w, block(bl, PB)], hrecv.at[w, hi], wh_sems, (w, d - 1), hi_peers[d - 1]
+                    zpart.at[span[w], block(bl, PB)],
+                    hrecv.at[i, span[w]],
+                    wh_sems.at[0, w],
+                    wh_sems.at[1, w],
+                    to,
                 )
-                for d in range(1, C)
-            ]
-            for cp in hc:
-                cp.wait()
-            total = hrecv[w, 0]
-            for i in range(1, C):
-                total = total + hrecv[w, i]
-        fin[w, here, :] = total.astype(BF)
-        return [
-            send(fin.at[w, here], fin.at[w, here], w_sems, (w, 2, i), dv_)
-            for i, (_, dv_) in enumerate(b_peers)
-        ]
-
-    def w_gather(w, copies):
-        for cp in copies:
-            cp.wait()
-        here = block(al, PA)
-        return [
-            send(fin.at[w, here], fin.at[w, here], w_sems, (w, 3, i), dv_)
-            for i, (_, dv_) in enumerate(a_peers)
-        ]
-
-    def w_keep(w, copies):
-        for cp in copies:
-            cp.wait()
-        store(fin.at[w], fin_hbm.at[w])
+            wait_both(hrecv.at[:, span[w]], wh_sems, (w,))
+            for kind in kinds_of[w]:
+                for i in range(C - 1):
+                    totals[kind] = totals[kind] + hrecv[i, kind]
+        for kind in kinds_of[w]:
+            fin[kind, here, :] = totals[kind].astype(BF)
+        for i, (_, to) in enumerate(b_peers):
+            send(
+                fin.at[span[w], here],
+                fin.at[span[w], here],
+                w_sems.at[0, w, 2],
+                w_sems.at[1, w, 2],
+                to,
+            )
+
+    def w_gather(w):
+        wait_both(fin.at[span[w], pl.ds(0, (B - 1) * PB)], w_sems, (w, 2))
+        for i, (_, to) in enumerate(a_peers):
+            send(
+                fin.at[span[w], block(al, PA)],
+                fin.at[span[w], block(al, PA)],
+                w_sems.at[0, w, 3],
+                w_sems.at[1, w, 3],
+                to,
+            )
+
+    def w_keep(w):
+        wait_both(fin.at[span[w], pl.ds(0, (A - 1) * PA)], w_sems, (w, 3))
+        store(fin.at[span[w]], fin_hbm.at[span[w]])
 
     weight_grads((GATE,))
-    gate_copies = w_scatter(GATE)
-    mix_copy.wait_recv()
+    bytes_of(mixo, mix_sems.at[1])
     out_grads()
-    out_copies = w_scatter(OUT)
+    w_scatter(GATEOUT)
 
     BU = 4
 
     def backward_block(i, _):
+        @pl.when(i == 1)
+        def _():
+            ar_middle(1)
+
+        @pl.when(i == 3)
+        def _():
+            ar_gather(1)
+
         chains = [(block(i * BU + u, NODES), i * BU + u, p) for u in range(BU) for p in range(PAIRS)]
         outs, dps = [], []
         for r, s, p in chains:
@@ -619,16 +660,12 @@
             low4[QUERY, r, ls] = (dq[r, ls] + got).astype(BF)
         return 0
 
-    FIRST = NB // BU // 2
-    lax.fori_loop(0, FIRST, backward_block, 0)
-    ar1 = ar_reduce(1, ar1)
-    lax.fori_loop(FIRST, NB // BU, backward_block, 0)
-    gate_copies = w_middle(GATE, gate_copies)
-    out_copies = w_middle(OUT, out_copies)
+    lax.fori_loop(0, NB // BU, backward_block, 0)
+    w_middle(GATEOUT)
     weight_grads((QUERY,))
-    query_copies = w_scatter(QUERY)
-
-    mats, totals = ar_result(1, ar1)
+    w_scatter(QUERIES)
+
+    mats, totals = ar_result(1)
     dsum = [m.astype(BF) for m in mats]
 
     KU = 4
@@ -646,10 +683,10 @@
 
     lax.fori_loop(0, NB // KU, key_block, 0)
     weight_grads((KEY, VALUE))
-    key_copies = w_scatter(KEY)
-    value_copies = w_scatter(VALUE)
-    gate_copies = w_spread(GATE, gate_copies)
-    out_copies = w_spread(OUT, out_copies)
+    w_scatter(KEYVALUE)
+    w_spread(GATEOUT)
+
+    DC = 4
 
     def normed_block(b, _):
         r = block(b, RB)
@@ -666,26 +703,24 @@
         s1 = jnp.sum(sa, axis=1, keepdims=True) + jnp.sum(sb, axis=1, keepdims=True)
         s2 = jnp.sum(sa * ha, axis=1, keepdims=True) + jnp.sum(sb * hb, axis=1, keepdims=True)
         st_send[r, :] = jnp.where(lane_half, s1, s2)
+
+        @pl.when(lax.rem(b, NR // DC) == NR // DC - 1)
+        def _():
+            i = b // (NR // DC)
+            piece = block(i, R // DC)
+            send(dn_send.at[piece], dn_recv.at[piece], dn_sems.at[0, 0], dn_sems.at[0, 2 + i], partner)
+            send(st_send.at[piece], st_recv.at[piece], dn_sems.at[0, 1], dn_sems.at[1, 2 + i], partner)
+
+        @pl.when(b == NR // 2)
+        def _():
+            w_middle(QUERIES)
+
         return 0
 
-    DC = 4
-    dn_copies = []
-    for i in range(DC):
-        lax.fori_loop(i * (NR // DC), (i + 1) * (NR // DC), normed_block, 0)
-        piece = pl.ds(i * (R // DC), R // DC)
-        dn_copies.append(
-            (
-                send(dn_send.at[piece], dn_recv.at[piece], dn_sems, (0, i), partner),
-                send(st_send.at[piece], st_recv.at[piece], dn_sems, (1, i), partner),
-            )
-        )
-        if i == 1:
-            query_copies = w_middle(QUERY, query_copies)
-    key_copies = w_middle(KEY, key_copies)
-    value_copies = w_middle(VALUE, value_copies)
-    query_copies = w_spread(QUERY, query_copies)
-    gate_copies = w_gather(GATE, gate_copies)
-    out_copies = w_gather(OUT, out_copies)
+    lax.fori_loop(0, NR, normed_block, 0)
+    w_middle(KEYVALUE)
+    w_spread(QUERIES)
+    w_gather(GATEOUT)
 
     def out_block(b, _):
         r = block(b, RB)
@@ -695,11 +730,17 @@
 
     lax.fori_loop(0, NR, out_block, 0)
     store(mixo, layer_out)
-    key_copies = w_spread(KEY, key_copies)
-    value_copies = w_spread(VALUE, value_copies)
-    query_copies = w_gather(QUERY, query_copies)
+    w_spread(KEYVALUE)
+    w_gather(QUERIES)
 
     def input_block(b, carry):
+        @pl.when(lax.rem(b, NR // DC) == 0)
+        def _():
+            i = b // (NR // DC)
+            piece = block(i, R // DC)
+            bytes_of(dn_recv.at[piece], dn_sems.at[0, 2 + i])
+            bytes_of(st_recv.at[piece], dn_sems.at[1, 2 + i])
+
         gain_sum, bias_sum = carry
         r = block(b, RB)
         dn = dn_own[r, :] + dn_recv[r, :]
@@ -717,51 +758,47 @@
         )
 
     carry = (jnp.zeros((1, W), F32), jnp.zeros((1, W), F32))
-    for i in range(DC):
-        for cp in dn_copies[i]:
-            cp.wait_recv()
-        carry = lax.fori_loop(i * (NR // DC), (i + 1) * (NR // DC), input_block, carry)
-        piece = pl.ds(i * (R // DC), R // DC)
-        store(co.at[piece], input_grad.at[piece])
+    carry = lax.fori_loop(0, NR, input_block, carry)
+    store(co, input_grad)
 
     row = lax.broadcasted_iota(jnp.int32, (8, W), 0)
-    terms = jnp.where(row == 0, carry[0], jnp.where(row == 1, carry[1], 0.0))
-    gb_part[...] = terms
-    gb_recv[pl.ds(lo, 1)] = terms[None]
-    gb_copies = [
-        send(gb_part, gb_recv.at[lo], gb_sems, (d - 1,), lo_peers[d - 1]) for d in range(1, L)
-    ]
-    key_copies = w_gather(KEY, key_copies)
-    value_copies = w_gather(VALUE, value_copies)
-    for cp in gb_copies:
-        cp.wait()
-    total = gb_recv[0]
-    for i in range(1, L):
-        total = total + gb_recv[i]
+    total = jnp.where(row == 0, carry[0], jnp.where(row == 1, carry[1], 0.0))
+
+    def in_order(total, step, held, index, count, peers):
+        gb_part[step] = total
+        held[pl.ds(index, 1)] = total[None]
+        for _, to in peers:
+            send(gb_part.at[step], held.at[index], gb_sems.at[0, step], gb_sems.at[1, step], to)
+        return count
+
+    def added(step, held, count):
+        wait_both(held.at[pl.ds(0, count - 1)], gb_sems, (step,))
+        total = held[0]
+        for i in range(1, count):
+            total = total + held[i]
+        return total
+
+    in_order(total, 0, gb_recv, al, A, a_peers)
+    w_gather(KEYVALUE)
+    in_order(added(0, gb_recv, A), 1, gb_z, bl, B, b_peers)
+    w_keep(GATEOUT)
+    w_keep(QUERIES)
+    total = added(1, gb_z, B)
     if C > 1:
-        gb_part[...] = total
-        gb_hi[pl.ds(hi, 1)] = total[None]
-        hc = [send(gb_part, gb_hi.at[hi], gbh_sems, (d - 1,), hi_peers[d - 1]) for d in range(1, C)]
-        for cp in hc:
-            cp.wait()
-        total = gb_hi[0]
-        for i in range(1, C):
-            total = total + gb_hi[i]
+        in_order(total, 2, gb_hi, hi, C, h_peers)
+        total = added(2, gb_hi, C)
     gain_grad[...] = total[0:1].reshape(W)
     bias_grad[...] = total[1:2].reshape(W)
-    w_keep(GATE, gate_copies)
-    w_keep(OUT, out_copies)
-    w_keep(QUERY, query_copies)
-    w_keep(KEY, key_copies)
-    w_keep(VALUE, value_copies)
+    w_keep(KEYVALUE)
     for cp in stores:
         cp.wait()
-    for cp in core_copies:
-        cp.wait_send()
-    mix_copy.wait_send()
-    for pair in dn_copies:
-        for cp in pair:
-            cp.wait_send()
+    bytes_of(gbs, core_sems.at[0, 0])
+    bytes_of(woo, core_sems.at[0, 1])
+    bytes_of(c, core_sems.at[0, 2])
+    bytes_of(x, core_sems.at[0, 3])
+    bytes_of(mix, mix_sems.at[0])
+    bytes_of(dn_send, dn_sems.at[0, 0])
+    bytes_of(st_send, dn_sems.at[0, 1])
 
 
 def shards(
@@ -780,12 +817,11 @@
     training_period,
 ):
     A, B, C = groups
-    L = A * B
     R, W = node_input.shape
     D = 2 * W
     NB = R // NODES
     PAIRS = W // 128
-    PER = CHUNKS // L
+    SR = 64 * PAIRS // A + 8
     PA = D // A
     PB = PA // B
     VM = pltpu.VMEM
@@ -840,31 +876,32 @@
             VM((R, W), F32),
             VM((R, 128), F32),
             VM((R, 128), F32),
-            VM((2, CHUNKS, 16, 128), F32),
-            VM((2, L, PER, 16, 128), F32),
-            VM((2, PER, 16, 128), F32),
-            VM((2, C, PER, 16, 128), F32),
-            VM((2, CHUNKS, 8, 128), F32),
+            VM((2, A, SR, 128), F32),
+            VM((2, A - 1, SR, 128), F32),
+            VM((2, SR, 128), F32),
+            VM((2, B - 1, SR, 128), F32),
+            VM((2, max(C - 1, 1), SR, 128), F32),
+            VM((2, A, SR, 128), F32),
             VM((5, D, W), F32),
             VM((5, D, W), BF),
-            VM((5, A - 1, PA, W), BF),
+            VM((A - 1, 5, PA, W), BF),
             VM((5, PA, W), F32),
-            VM((5, B - 1, PB, W), F32),
-            VM((5, C, PB, W), F32),
-            VM((8, W), F32),
-            VM((L, 8, W), F32),
+            VM((B - 1, 5, PB, W), F32),
+            VM((max(C - 1, 1), 5, PB, W), F32),
+            VM((3, 8, W), F32),
+            VM((A, 8, W), F32),
+            VM((B, 8, W), F32),
             VM((C, 8, W), F32),
             dma((15,)),
-            dma((10,)),
-            dma((2, 8)),
-            dma((2, 1)),
-            dma((2, 2, 4)),
-            dma((2, 2, 2, L - 1)),
-            dma((2, 2, max(C - 1, 1))),
-            dma((2, 5, 4, max(A, B) - 1)),
-            dma((2, 5, max(C - 1, 1))),
-            dma((2, L - 1)),
-            dma((2, max(C - 1, 1))),
+            dma((8,)),
+            dma((2, 7)),
+            dma((2,)),
+            dma((2, 6)),
+            dma((2, 2, 3)),
+            dma((2, 2)),
+            dma((2, 3, 4)),
+            dma((2, 3)),
+            dma((2, 3)),
         ],
         compiler_params=pltpu.CompilerParams(
             collective_id=0, has_side_effects=True, vmem_limit_bytes=63 << 20

time: 83.9 us -> 80.4 us (0.958)
  Pallas kernels: 82.9 us -> 79.6 us
    pallas_call x1, Pallas kernels: 78.4 us -> 75 us  [shards(): pl.pallas_call(functools.partial(layer_kernel, groups), name='layer_kerne...]
where the time goes in v3:
time: 80.4 us; the launch traced here: 80.2 us
  Pallas kernels  79.6 us (99%)
    pallas_call x1, Pallas kernels, shards(): pl.pallas_call(functools.partial(layer_kernel, groups), name='layer_kerne...  75 us
    pallas_call x1, Pallas kernels, shards(): pl.pallas_call(finish_kernel, name='finish_kernel', out_shape=(jax.ShapeD...  4.54 us

profile of v3, /device:TPU:0, one launch (start us, length us, event | category | flops | bytes accessed | tf_op | source)
XLA Modules:
  0.0 80.2 jit_solution(13545863471869335062)
XLA Ops:
  0.6 75.0 %layer_kernel.1 = (bf16[2048,256]{1,0:T(8,128)(2,1)}, bf16[2048,256]{1,0:T(8,128)(2,1)}, f32[256]{0:T(256)}, f32[256]{0:T(256)}, bf16[5,512,256]{2,1,0:T(8,128)(2,1)}) custom-call(bf16[2048,256]{1,0:T(8,128)(2,1)} %x_hbm.1, bf16[2048,256]{1,0:T(8,128)(2,1)} %c_hbm.1, bf16[256]{0:T(256)(128)(2,1)} %gain.1, bf16[256]{0:T(256)(128)(2,1)} %bias.1, ...), custom_call_target="tpu_custom_call" | custom-call | tf_op jit(solution)/shard_map/layer_kernel/pallas_call | solution.py:832
  75.7 4.5 %finish_kernel.1 = (bf16[2048,256]{1,0:T(8,128)(2,1)}, bf16[2048,256]{1,0:T(8,128)(2,1)}, f32[256]{0:T(256)}, f32[256]{0:T(256)}, f32[512,256]{1,0:T(8,128)}, /*...) custom-call(bf16[2048,256]{1,0:T(8,128)(2,1)} %get-tuple-element.14.lo_in, ...), custom_call_target="tpu_custom_call" | custom-call | tf_op jit(solution)/shard_map/finish_kernel/pallas_call | solution.py:923

commit v4 on v3

--- a/solution.py
+++ b/solution.py
@@ -50,27 +50,34 @@
     groups,
     x_hbm,
     c_hbm,
-    gain,
-    bias,
+    gain_hbm,
+    bias_hbm,
     wq,
     wk,
     wv,
     wg,
     wo_hbm,
     adjacent_hbm,
-    tally,
-    period,
+    tally_hbm,
+    period_hbm,
     layer_out,
     input_grad,
     gain_grad,
     bias_grad,
     fin_hbm,
+    gain,
+    bias,
+    gain_out,
+    bias_out,
+    tally,
+    period,
     x,
     xo,
     c,
     co,
     wo,
     adjacent,
+    weight,
     fin,
     gbs,
     gbo,
@@ -181,7 +188,10 @@
         loads.append(copy)
         return copy
 
-    XC = 4
+    RB = 1024
+    NR = R // RB
+    XC = NR
+    adjacent_load = load(adjacent_hbm, adjacent)
     x_loads = []
     for i in range(XC):
         piece = pl.ds(i * (R // XC), R // XC)
@@ -193,7 +203,6 @@
         cols = pl.ds(i * W, W)
         w_loads.append(load(w.at[own_rows], wall.at[pl.ds(0, W), cols]))
         w_loads.append(load(w.at[oth_rows], wall.at[pl.ds(W, W), cols]))
-    adjacent_load = load(adjacent_hbm, adjacent)
 
     stores = []
 
@@ -202,8 +211,28 @@
         copy.start()
         stores.append(copy)
 
+    small_loads = [
+        load(gain_hbm, gain),
+        load(bias_hbm, bias),
+        load(tally_hbm, tally),
+        load(period_hbm, period),
+    ]
+    for cp in small_loads:
+        cp.wait()
     gbs[0:8, :] = jnp.broadcast_to(gain[...].astype(F32).reshape(1, W), (8, W))
     gbs[8:16, :] = jnp.broadcast_to(bias[...].astype(F32).reshape(1, W), (8, W))
+    node_of = lax.broadcasted_iota(jnp.int32, (NODES, 128), 0)
+    def count_block(i, _):
+        for s in (2 * i, 2 * i + 1):
+            listed = adjacent[:, block(s, NODES)]
+            count = jnp.zeros((NODES, NODES), F32)
+            for j in range(listed.shape[0]):
+                count = count + jnp.where(listed[j : j + 1, :] == node_of, 1.0, 0.0)
+            weight[s] = jnp.where(
+                count > 0.0, jnp.log(jnp.maximum(count, 1.0)) * LOG2E, -1e30
+            )
+        return 0
+
     pl.semaphore_wait(barrier, len(greeted))
 
     send(gbs, gbo, core_sems.at[0, 0], core_sems.at[1, 0], partner)
@@ -216,22 +245,19 @@
     c_load.wait()
     send(c, co, core_sems.at[0, 2], core_sems.at[1, 2], partner)
 
-    RB = 256
-    NR = R // RB
-
     def own_dmix(b, _):
         r = block(b, RB)
         dmix[r, :] = nt(c[r, :], wo[own_rows, :])
         return 0
 
     lax.fori_loop(0, NR, own_dmix, 0)
+
 
     sum_part[...] = jnp.zeros_like(sum_part)
     bytes_of(gbo, core_sems.at[1, 0])
     gain_own, bias_own = gbs[0:1, :], gbs[8:9, :]
     gain_oth, bias_oth = gbo[0:1, :], gbo[8:9, :]
     lane_half = lax.broadcasted_iota(jnp.int32, (1, 128), 1) < 64
-    node_of = lax.broadcasted_iota(jnp.int32, (NODES, 128), 0)
 
     def live_rows(first, a, count):
         node = lax.broadcasted_iota(jnp.int32, (NODES, a.shape[1]), 0)
@@ -393,6 +419,9 @@
 
     lax.fori_loop(0, NR, gate_block, 0)
     ar_middle(0)
+    adjacent_load.wait()
+    lax.fori_loop(0, NB // 2, count_block, 0)
+    ar_gather(0)
 
     half_row = jnp.where(lane_half, 1.0, 0.0)
     half_a = jnp.broadcast_to(half_row, (NODES, 128)).astype(BF)
@@ -404,23 +433,11 @@
     def joined(a):
         return jnp.where(lane_half, a[0:NODES], a[NODES : 2 * NODES])
 
-    FU = 4
+    FU = 8
     lanes = [slice(p * 128, (p + 1) * 128) for p in range(PAIRS)]
 
     def forward_block(i, _):
-        @pl.when(i == NB // FU // 2)
-        def _():
-            ar_gather(0)
-
         chains = [(i * FU + u, p) for u in range(FU) for p in range(PAIRS)]
-        weights = []
-        for u in range(FU):
-            listed = adjacent[:, block(i * FU + u, NODES)]
-            count = jnp.zeros((NODES, NODES), F32)
-            for j in range(listed.shape[0]):
-                count = count + jnp.where(listed[j : j + 1, :] == node_of, 1.0, 0.0)
-            weight = jnp.where(count > 0.0, jnp.log(jnp.maximum(count, 1.0)) * LOG2E, -1e30)
-            weights.append(lanes_cat(weight, weight))
         scores = []
         for s, p in chains:
             r, ls = block(s, NODES), lanes[p]
@@ -431,7 +448,8 @@
             )
         probs = []
         for j, score in enumerate(scores):
-            score = score + weights[j // PAIRS]
+            bias = weight[chains[j][0]]
+            score = score + lanes_cat(bias, bias)
             e = jnp.exp2(score - jnp.max(score, axis=0, keepdims=True))
             probs.append(split(e * (1.0 / jnp.sum(e, axis=0, keepdims=True))))
         for (s, p), (high, low) in zip(chains, probs):
@@ -447,7 +465,6 @@
             att[r, ls] = joined(o[:, 0:128] + o[:, 128:256])
         return 0
 
-    adjacent_load.wait()
     lax.fori_loop(0, NB // FU, forward_block, 0)
 
     mats, totals = ar_result(0)
@@ -464,7 +481,7 @@
         den_w.append(rows_cat(th, tl))
         back_w.append(lanes_cat(sh, sh, sl))
 
-    GU = 4
+    GU = 8
 
     def glob_block(i, carry):
         r = block(i, GU * NODES)
@@ -498,7 +515,7 @@
     ar_scatter(1)
     send(mix, mixo, mix_sems.at[0], mix_sems.at[1], partner)
 
-    KB = 512
+    KB = 1024
 
     def weight_grads(kinds):
         def step(i, _):
@@ -529,9 +546,8 @@
     PA = D // A
     PB = PA // B
 
-    QUERIES, KEYVALUE, GATEOUT = 0, 1, 2
-    span = {QUERIES: pl.ds(0, 1), KEYVALUE: pl.ds(1, 2), GATEOUT: pl.ds(3, 2)}
-    kinds_of = {QUERIES: (QUERY,), KEYVALUE: (KEY, VALUE), GATEOUT: (GATE, OUT)}
+    kinds_of = {w: (w,) for w in range(5)}
+    span = {w: pl.ds(w, 1) for w in range(5)}
 
     def w_scatter(w):
         for kind in kinds_of[w]:
@@ -613,9 +629,10 @@
         store(fin.at[span[w]], fin_hbm.at[span[w]])
 
     weight_grads((GATE,))
+    w_scatter(GATE)
     bytes_of(mixo, mix_sems.at[1])
     out_grads()
-    w_scatter(GATEOUT)
+    w_scatter(OUT)
 
     BU = 4
 
@@ -623,6 +640,10 @@
         @pl.when(i == 1)
         def _():
             ar_middle(1)
+
+        @pl.when(i == 2)
+        def _():
+            w_middle(GATE)
 
         @pl.when(i == 3)
         def _():
@@ -661,14 +682,15 @@
         return 0
 
     lax.fori_loop(0, NB // BU, backward_block, 0)
-    w_middle(GATEOUT)
+    w_middle(OUT)
     weight_grads((QUERY,))
-    w_scatter(QUERIES)
+    w_scatter(QUERY)
+    w_spread(GATE)
 
     mats, totals = ar_result(1)
     dsum = [m.astype(BF) for m in mats]
 
-    KU = 4
+    KU = 8
 
     def key_block(i, _):
         r = block(i, KU * NODES)
@@ -682,11 +704,13 @@
         return 0
 
     lax.fori_loop(0, NB // KU, key_block, 0)
-    weight_grads((KEY, VALUE))
-    w_scatter(KEYVALUE)
-    w_spread(GATEOUT)
-
-    DC = 4
+    weight_grads((KEY,))
+    w_scatter(KEY)
+    weight_grads((VALUE,))
+    w_scatter(VALUE)
+    w_spread(OUT)
+
+    DC = NR
 
     def normed_block(b, _):
         r = block(b, RB)
@@ -713,14 +737,12 @@
 
         @pl.when(b == NR // 2)
         def _():
-            w_middle(QUERIES)
+            w_middle(QUERY)
 
         return 0
 
     lax.fori_loop(0, NR, normed_block, 0)
-    w_middle(KEYVALUE)
-    w_spread(QUERIES)
-    w_gather(GATEOUT)
+    w_middle(KEY)
 
     def out_block(b, _):
         r = block(b, RB)
@@ -730,8 +752,11 @@
 
     lax.fori_loop(0, NR, out_block, 0)
     store(mixo, layer_out)
-    w_spread(KEYVALUE)
-    w_gather(QUERIES)
+    w_middle(VALUE)
+    w_gather(GATE)
+    w_gather(OUT)
+    w_spread(QUERY)
+    w_spread(KEY)
 
     def input_block(b, carry):
         @pl.when(lax.rem(b, NR // DC) == 0)
@@ -760,6 +785,9 @@
     carry = (jnp.zeros((1, W), F32), jnp.zeros((1, W), F32))
     carry = lax.fori_loop(0, NR, input_block, carry)
     store(co, input_grad)
+    w_spread(VALUE)
+    w_gather(QUERY)
+    w_gather(KEY)
 
     row = lax.broadcasted_iota(jnp.int32, (8, W), 0)
     total = jnp.where(row == 0, carry[0], jnp.where(row == 1, carry[1], 0.0))
@@ -779,17 +807,21 @@
         return total
 
     in_order(total, 0, gb_recv, al, A, a_peers)
-    w_gather(KEYVALUE)
+    w_gather(VALUE)
     in_order(added(0, gb_recv, A), 1, gb_z, bl, B, b_peers)
-    w_keep(GATEOUT)
-    w_keep(QUERIES)
+    w_keep(GATE)
+    w_keep(OUT)
+    w_keep(QUERY)
     total = added(1, gb_z, B)
     if C > 1:
         in_order(total, 2, gb_hi, hi, C, h_peers)
         total = added(2, gb_hi, C)
-    gain_grad[...] = total[0:1].reshape(W)
-    bias_grad[...] = total[1:2].reshape(W)
-    w_keep(KEYVALUE)
+    gain_out[...] = total[0:1].reshape(W)
+    bias_out[...] = total[1:2].reshape(W)
+    store(gain_out, gain_grad)
+    store(bias_out, bias_grad)
+    w_keep(KEY)
+    w_keep(VALUE)
     for cp in stores:
         cp.wait()
     bytes_of(gbs, core_sems.at[0, 0])
@@ -826,8 +858,6 @@
     PB = PA // B
     VM = pltpu.VMEM
     dma = pltpu.SemaphoreType.DMA
-    vmem = pl.BlockSpec(memory_space=pltpu.VMEM)
-    smem = pl.BlockSpec(memory_space=pltpu.SMEM)
     hbm = pl.BlockSpec(memory_space=pl.ANY)
     layer_output, input_grad, gain_grad, bias_grad, fin = pl.pallas_call(
         functools.partial(layer_kernel, groups),
@@ -839,15 +869,22 @@
             jax.ShapeDtypeStruct((W,), F32),
             jax.ShapeDtypeStruct((5, D, W), BF),
         ),
-        in_specs=[hbm] * 2 + [vmem] * 2 + [hbm] * 6 + [smem] * 2,
-        out_specs=(hbm, hbm, vmem, vmem, hbm),
+        in_specs=[hbm] * 12,
+        out_specs=(hbm,) * 5,
         scratch_shapes=[
+            VM((W,), BF),
+            VM((W,), BF),
+            VM((W,), F32),
+            VM((W,), F32),
+            pltpu.SMEM((NB,), jnp.int32),
+            pltpu.SMEM((NB,), jnp.int32),
             VM((R, W), BF),
             VM((R, W), BF),
             VM((R, W), BF),
             VM((R, W), BF),
             VM((D, W), BF),
             VM((adjacent_vertices.shape[1], R), jnp.int32),
+            VM((NB, NODES, NODES), F32),
             VM((5, D, W), BF),
             VM((16, W), F32),
             VM((16, W), F32),
@@ -892,15 +929,15 @@
             VM((A, 8, W), F32),
             VM((B, 8, W), F32),
             VM((C, 8, W), F32),
-            dma((15,)),
-            dma((8,)),
+            dma((20,)),
+            dma((10,)),
             dma((2, 7)),
             dma((2,)),
             dma((2, 6)),
             dma((2, 2, 3)),
             dma((2, 2)),
-            dma((2, 3, 4)),
-            dma((2, 3)),
+            dma((2, 5, 4)),
+            dma((2, 5)),
             dma((2, 3)),
         ],
         compiler_params=pltpu.CompilerParams(
@@ -930,36 +967,47 @@
             jax.ShapeDtypeStruct((W,), F32),
         )
         + tuple(jax.ShapeDtypeStruct((D, W), F32) for _ in range(5)),
-        in_specs=[hbm, hbm, vmem, vmem, hbm],
-        out_specs=(hbm, hbm, vmem, vmem) + (hbm,) * 5,
-        scratch_shapes=[VM((5, D, W), BF), VM((5, D, W), F32), VM((2, R, W), BF), dma((14,))],
+        in_specs=[hbm] * 5,
+        out_specs=(hbm,) * 9,
+        scratch_shapes=[
+            VM((5, D, W), BF),
+            VM((5, D, W), F32),
+            VM((2, R, W), BF),
+            VM((W,), F32),
+            VM((W,), F32),
+            dma((18,)),
+        ],
     )(layer_output, input_grad, gain_grad, bias_grad, fin)
 
 
 def finish_kernel(
-    lo_in, ig_in, gain_in, bias_in, fin, lo, ig, gain, bias, gq, gk, gv, gg, go, low, full, wide, sems
+    lo_in, ig_in, gain_in, bias_in, fin, lo, ig, gain, bias, gq, gk, gv, gg, go, *scratch
 ):
-    loads = []
+    low, full, wide, gain_here, bias_here, sems = scratch
+    loads, stores = [], []
 
     def begin(src, dst, into):
-        copy = pltpu.make_async_copy(src, dst, sems.at[len(into) + (0 if into is loads else 7)])
+        copy = pltpu.make_async_copy(src, dst, sems.at[len(into) + (0 if into is loads else 9)])
         copy.start()
         into.append(copy)
 
     for i in range(5):
         begin(fin.at[i], low.at[i], loads)
-    begin(lo_in, wide.at[0], loads)
-    begin(ig_in, wide.at[1], loads)
-    gain[...] = gain_in[...]
-    bias[...] = bias_in[...]
-    stores = []
+    straight = (
+        (lo_in, wide.at[0], lo),
+        (ig_in, wide.at[1], ig),
+        (gain_in, gain_here, gain),
+        (bias_in, bias_here, bias),
+    )
+    for src, here, _ in straight:
+        begin(src, here, loads)
     for i, out in enumerate((gq, gk, gv, gg, go)):
         loads[i].wait()
         full[i] = low[i].astype(F32)
         begin(full.at[i], out, stores)
-    for i, out in enumerate((lo, ig)):
+    for i, (_, here, out) in enumerate(straight):
         loads[5 + i].wait()
-        begin(wide.at[i], out, stores)
+        begin(here, out, stores)
     for cp in stores:
         cp.wait()
 

time: 80.4 us -> 74.1 us (0.922)
  Pallas kernels: 79.6 us -> 73.2 us
    pallas_call x1, Pallas kernels: 75 us -> 69.8 us  [shards(): pl.pallas_call(functools.partial(layer_kernel, groups), name='layer_kerne...]
    pallas_call x1, Pallas kernels: 4.54 us -> 3.33 us  [shards(): pl.pallas_call(finish_kernel, name='finish_kernel', out_shape=(jax.ShapeD...]
where the time goes in v4:
time: 74.1 us; the launch traced here: 74 us
  Pallas kernels  73.2 us (99%)
  between operations  0.82 us (1%)
    pallas_call x1, Pallas kernels, shards(): pl.pallas_call(functools.partial(layer_kernel, groups), name='layer_kerne...  69.8 us
    pallas_call x1, Pallas kernels, shards(): pl.pallas_call(finish_kernel, name='finish_kernel', out_shape=(jax.ShapeD...  3.33 us

profile of v4, /device:TPU:0, one launch (start us, length us, event | category | flops | bytes accessed | tf_op | source)
XLA Modules:
  0.0 74.0 jit_solution(15661184942779784752)
XLA Ops:
  0.6 69.8 %layer_kernel.1 = (bf16[2048,256]{1,0:T(8,128)(2,1)}, bf16[2048,256]{1,0:T(8,128)(2,1)}, f32[256]{0:T(256)}, f32[256]{0:T(256)}, bf16[5,512,256]{2,1,0:T(8,128)(2,1)}) custom-call(bf16[2048,256]{1,0:T(8,128)(2,1)} %x_hbm.1, bf16[2048,256]{1,0:T(8,128)(2,1)} %c_hbm.1, bf16[256]{0:T(256)(128)(2,1)} %gain_hbm.1, bf16[256]{0:T(256)(128)(2,1)} %bias_hbm.1, ...), custom_call_target="tpu_custom_call" | custom-call | tf_op jit(solution)/shard_map/layer_kernel/pallas_call | solution.py:862
  70.5 3.3 %finish_kernel.1 = (bf16[2048,256]{1,0:T(8,128)(2,1)}, bf16[2048,256]{1,0:T(8,128)(2,1)}, f32[256]{0:T(256)}, f32[256]{0:T(256)}, f32[512,256]{1,0:T(8,128)}, /*...) custom-call(bf16[2048,256]{1,0:T(8,128)(2,1)} %get-tuple-element.14.lo_in, ...), custom_call_target="tpu_custom_call" | custom-call | tf_op jit(solution)/shard_map/finish_kernel/pallas_call | solution.py:960

commit v5 on v4

--- a/solution.py
+++ b/solution.py
@@ -223,11 +223,16 @@
     gbs[8:16, :] = jnp.broadcast_to(bias[...].astype(F32).reshape(1, W), (8, W))
     node_of = lax.broadcasted_iota(jnp.int32, (NODES, 128), 0)
     def count_block(i, _):
+        node = node_of.astype(F32).astype(BF)
+        one = jnp.ones((NODES, NODES), BF)
+        zero = jnp.zeros((NODES, NODES), BF)
         for s in (2 * i, 2 * i + 1):
-            listed = adjacent[:, block(s, NODES)]
-            count = jnp.zeros((NODES, NODES), F32)
+            listed = adjacent[:, block(s, NODES)].astype(F32).astype(BF)
+            count = zero
             for j in range(listed.shape[0]):
-                count = count + jnp.where(listed[j : j + 1, :] == node_of, 1.0, 0.0)
+                same = jnp.broadcast_to(listed[j : j + 1, :], (NODES, NODES)) == node
+                count = count + jnp.where(same, one, zero)
+            count = count.astype(F32)
             weight[s] = jnp.where(
                 count > 0.0, jnp.log(jnp.maximum(count, 1.0)) * LOG2E, -1e30
             )
@@ -245,13 +250,8 @@
     c_load.wait()
     send(c, co, core_sems.at[0, 2], core_sems.at[1, 2], partner)
 
-    def own_dmix(b, _):
-        r = block(b, RB)
-        dmix[r, :] = nt(c[r, :], wo[own_rows, :])
-        return 0
-
-    lax.fori_loop(0, NR, own_dmix, 0)
-
+    adjacent_load.wait()
+    lax.fori_loop(0, NB // 2, count_block, 0)
 
     sum_part[...] = jnp.zeros_like(sum_part)
     bytes_of(gbo, core_sems.at[1, 0])
@@ -412,16 +412,13 @@
         qh[r, :], ql[r, :] = split(qq * (0.125 * LOG2E))
         gg = nn(n, wall[:, 3 * W : 4 * W])
         g[r, :] = gg
-        dm = dmix[r, :] + nt(co[r, :], woo[...])
+        dm = nt(lanes_cat(c[r, :], co[r, :]), lanes_cat(wo[own_rows, :], woo[...]))
         dmix[r, :] = dm
         datt[r, :] = dm * ((1.0 - BETA) * gg + BETA)
         return 0
 
     lax.fori_loop(0, NR, gate_block, 0)
     ar_middle(0)
-    adjacent_load.wait()
-    lax.fori_loop(0, NB // 2, count_block, 0)
-    ar_gather(0)
 
     half_row = jnp.where(lane_half, 1.0, 0.0)
     half_a = jnp.broadcast_to(half_row, (NODES, 128)).astype(BF)
@@ -433,10 +430,14 @@
     def joined(a):
         return jnp.where(lane_half, a[0:NODES], a[NODES : 2 * NODES])
 
-    FU = 8
+    FU = 4
     lanes = [slice(p * 128, (p + 1) * 128) for p in range(PAIRS)]
 
     def forward_block(i, _):
+        @pl.when(i == 3)
+        def _():
+            ar_gather(0)
+
         chains = [(i * FU + u, p) for u in range(FU) for p in range(PAIRS)]
         scores = []
         for s, p in chains:
@@ -546,87 +547,87 @@
     PA = D // A
     PB = PA // B
 
-    kinds_of = {w: (w,) for w in range(5)}
-    span = {w: pl.ds(w, 1) for w in range(5)}
+    B_FIRST = (QUERY,) if A == B else ()
+
+    def order(w):
+        first, second = (al, a_peers), (bl, b_peers)
+        return (second, first) if w in B_FIRST else (first, second)
 
     def w_scatter(w):
-        for kind in kinds_of[w]:
-            psend[kind] = part[kind].astype(BF)
-        for i, (j, to) in enumerate(a_peers):
+        psend[w] = part[w].astype(BF)
+        for i, (j, to) in enumerate(order(w)[0][1]):
             send(
-                psend.at[span[w], block(j, PA)],
-                precv.at[i, span[w]],
+                psend.at[w, block(j, PA)],
+                precv.at[w, i],
                 w_sems.at[0, w, 0],
                 w_sems.at[1, w, 0],
                 to,
             )
 
     def w_middle(w):
-        wait_both(precv.at[:, span[w]], w_sems, (w, 0))
-        for kind in kinds_of[w]:
-            total = part[kind, block(al, PA), :]
-            for i in range(A - 1):
-                total = total + precv[i, kind].astype(F32)
-            zpart[kind] = total
-        for i, (j, to) in enumerate(b_peers):
+        (mine, _), (_, peers) = order(w)
+        wait_both(precv.at[w], w_sems, (w, 0))
+        total = part[w, block(mine, PA), :]
+        for i in range(A - 1):
+            total = total + precv[w, i].astype(F32)
+        zpart[w] = total
+        for i, (j, to) in enumerate(peers):
             send(
-                zpart.at[span[w], block(j, PB)],
-                zrecv.at[i, span[w]],
+                zpart.at[w, block(j, PB)],
+                zrecv.at[w, i],
                 w_sems.at[0, w, 1],
                 w_sems.at[1, w, 1],
                 to,
             )
 
-    here = pl.ds(pl.multiple_of(al * PA + bl * PB, PB), PB)
+    def share(w):
+        (first, _), (second, _) = order(w)
+        return pl.ds(pl.multiple_of(first * PA + second * PB, PB), PB)
 
     def w_spread(w):
-        wait_both(zrecv.at[:, span[w]], w_sems, (w, 1))
-        totals = {}
-        for kind in kinds_of[w]:
-            total = zpart[kind, block(bl, PB), :]
-            for i in range(B - 1):
-                total = total + zrecv[i, kind]
-            totals[kind] = total
+        _, (mine, peers) = order(w)
+        wait_both(zrecv.at[w], w_sems, (w, 1))
+        total = zpart[w, block(mine, PB), :]
+        for i in range(B - 1):
+            total = total + zrecv[w, i]
         if C > 1:
-            for kind in kinds_of[w]:
-                zpart[kind, block(bl, PB), :] = totals[kind]
+            zpart[w, block(mine, PB), :] = total
             for i, (_, to) in enumerate(h_peers):
                 send(
-                    zpart.at[span[w], block(bl, PB)],
-                    hrecv.at[i, span[w]],
+                    zpart.at[w, block(mine, PB)],
+                    hrecv.at[w, i],
                     wh_sems.at[0, w],
                     wh_sems.at[1, w],
                     to,
                 )
-            wait_both(hrecv.at[:, span[w]], wh_sems, (w,))
-            for kind in kinds_of[w]:
-                for i in range(C - 1):
-                    totals[kind] = totals[kind] + hrecv[i, kind]
-        for kind in kinds_of[w]:
-            fin[kind, here, :] = totals[kind].astype(BF)
-        for i, (_, to) in enumerate(b_peers):
+            wait_both(hrecv.at[w], wh_sems, (w,))
+            for i in range(C - 1):
+                total = total + hrecv[w, i]
+        fin[w, share(w), :] = total.astype(BF)
+        for _, to in peers:
             send(
-                fin.at[span[w], here],
-                fin.at[span[w], here],
+                fin.at[w, share(w)],
+                fin.at[w, share(w)],
                 w_sems.at[0, w, 2],
                 w_sems.at[1, w, 2],
                 to,
             )
 
     def w_gather(w):
-        wait_both(fin.at[span[w], pl.ds(0, (B - 1) * PB)], w_sems, (w, 2))
-        for i, (_, to) in enumerate(a_peers):
+        mine, peers = order(w)[0]
+        wait_both(fin.at[w, pl.ds(0, (B - 1) * PB)], w_sems, (w, 2))
+        for _, to in peers:
             send(
-                fin.at[span[w], block(al, PA)],
-                fin.at[span[w], block(al, PA)],
+                fin.at[w, block(mine, PA)],
+                fin.at[w, block(mine, PA)],
                 w_sems.at[0, w, 3],
                 w_sems.at[1, w, 3],
                 to,
             )
 
     def w_keep(w):
-        wait_both(fin.at[span[w], pl.ds(0, (A - 1) * PA)], w_sems, (w, 3))
-        store(fin.at[span[w]], fin_hbm.at[span[w]])
+        wait_both(fin.at[w, pl.ds(0, (A - 1) * PA)], w_sems, (w, 3))
+        store(fin.at[w], fin_hbm.at[w])
 
     weight_grads((GATE,))
     w_scatter(GATE)
@@ -735,14 +736,11 @@
             send(dn_send.at[piece], dn_recv.at[piece], dn_sems.at[0, 0], dn_sems.at[0, 2 + i], partner)
             send(st_send.at[piece], st_recv.at[piece], dn_sems.at[0, 1], dn_sems.at[1, 2 + i], partner)
 
-        @pl.when(b == NR // 2)
-        def _():
-            w_middle(QUERY)
-
         return 0
 
     lax.fori_loop(0, NR, normed_block, 0)
     w_middle(KEY)
+    w_middle(QUERY)
 
     def out_block(b, _):
         r = block(b, RB)
@@ -755,8 +753,8 @@
     w_middle(VALUE)
     w_gather(GATE)
     w_gather(OUT)
+    w_spread(KEY)
     w_spread(QUERY)
-    w_spread(KEY)
 
     def input_block(b, carry):
         @pl.when(lax.rem(b, NR // DC) == 0)
@@ -786,7 +784,6 @@
     carry = lax.fori_loop(0, NR, input_block, carry)
     store(co, input_grad)
     w_spread(VALUE)
-    w_gather(QUERY)
     w_gather(KEY)
 
     row = lax.broadcasted_iota(jnp.int32, (8, W), 0)
@@ -808,6 +805,7 @@
 
     in_order(total, 0, gb_recv, al, A, a_peers)
     w_gather(VALUE)
+    w_gather(QUERY)
     in_order(added(0, gb_recv, A), 1, gb_z, bl, B, b_peers)
     w_keep(GATE)
     w_keep(OUT)
@@ -921,10 +919,10 @@
             VM((2, A, SR, 128), F32),
             VM((5, D, W), F32),
             VM((5, D, W), BF),
-            VM((A - 1, 5, PA, W), BF),
+            VM((5, A - 1, PA, W), BF),
             VM((5, PA, W), F32),
-            VM((B - 1, 5, PB, W), F32),
-            VM((max(C - 1, 1), 5, PB, W), F32),
+            VM((5, B - 1, PB, W), F32),
+            VM((5, max(C - 1, 1), PB, W), F32),
             VM((3, 8, W), F32),
             VM((A, 8, W), F32),
             VM((B, 8, W), F32),

time: 74.1 us -> 70.7 us (0.954)
  Pallas kernels: 73.2 us -> 69.9 us
    pallas_call x1, Pallas kernels: 69.8 us -> 66.6 us  [shards(): pl.pallas_call(functools.partial(layer_kernel, groups), name='layer_kerne...]
where the time goes in v5:
time: 70.7 us; the launch traced here: 70.6 us
  Pallas kernels  69.9 us (99%)
    pallas_call x1, Pallas kernels, shards(): pl.pallas_call(functools.partial(layer_kernel, groups), name='layer_kerne...  66.6 us
    pallas_call x1, Pallas kernels, shards(): pl.pallas_call(finish_kernel, name='finish_kernel', out_shape=(jax.ShapeD...  3.33 us

profile of v5, /device:TPU:0, one launch (start us, length us, event | category | flops | bytes accessed | tf_op | source)
XLA Modules:
  0.0 70.6 jit_solution(10423801975427165109)
XLA Ops:
  0.6 66.6 %layer_kernel.1 = (bf16[2048,256]{1,0:T(8,128)(2,1)}, bf16[2048,256]{1,0:T(8,128)(2,1)}, f32[256]{0:T(256)}, f32[256]{0:T(256)}, bf16[5,512,256]{2,1,0:T(8,128)(2,1)}) custom-call(bf16[2048,256]{1,0:T(8,128)(2,1)} %x_hbm.1, bf16[2048,256]{1,0:T(8,128)(2,1)} %c_hbm.1, bf16[256]{0:T(256)(128)(2,1)} %gain_hbm.1, bf16[256]{0:T(256)(128)(2,1)} %bias_hbm.1, ...), custom_call_target="tpu_custom_call" | custom-call | tf_op jit(solution)/shard_map/layer_kernel/pallas_call | solution.py:860
  67.2 3.3 %finish_kernel.1 = (bf16[2048,256]{1,0:T(8,128)(2,1)}, bf16[2048,256]{1,0:T(8,128)(2,1)}, f32[256]{0:T(256)}, f32[256]{0:T(256)}, f32[512,256]{1,0:T(8,128)}, /*...) custom-call(bf16[2048,256]{1,0:T(8,128)(2,1)} %get-tuple-element.14.lo_in, ...), custom_call_target="tpu_custom_call" | custom-call | tf_op jit(solution)/shard_map/finish_kernel/pallas_call | solution.py:958

commit v6 on v5

--- a/solution.py
+++ b/solution.py
@@ -100,6 +100,7 @@
     att,
     prob,
     dq,
+    dv,
     low4,
     mix,
     mixo,
@@ -173,7 +174,7 @@
         bytes_of(ref, sems.at[(0,) + index])
         bytes_of(ref, sems.at[(1,) + index])
 
-    dk, dv, dn_own, dn_send = att, q_sig, g, dmix
+    dk, dn_own, dn_send = att, g, dmix
 
     barrier = pltpu.get_barrier_semaphore()
     greeted = [partner] + [to for _, to in a_peers + b_peers + h_peers]
@@ -468,6 +469,21 @@
 
     lax.fori_loop(0, NB // FU, forward_block, 0)
 
+    def value_block(i, _):
+        chains = [(i * BU + u, p) for u in range(BU) for p in range(PAIRS)]
+        outs = []
+        for s, p in chains:
+            oh, ol = split(datt[block(s, NODES), lanes[p]])
+            outs.append((apart(oh), apart(ol)))
+        for (s, p), (oh, ol) in zip(chains, outs):
+            got = nn(prob[s, p, 0], lanes_cat(oh, ol))
+            got = got[:, 0:128] + got[:, 128:256] + nn(prob[s, p, 1], oh)
+            dv[block(s, NODES), lanes[p]] = got
+        return 0
+
+    BU = 4
+    lax.fori_loop(0, NB // BU, value_block, 0)
+
     mats, totals = ar_result(0)
     square = (2, 128, 128)
     same_head = (lax.broadcasted_iota(jnp.int32, (128, 128), 0) < 64) == (
@@ -635,8 +651,6 @@
     out_grads()
     w_scatter(OUT)
 
-    BU = 4
-
     def backward_block(i, _):
         @pl.when(i == 1)
         def _():
@@ -651,21 +665,17 @@
             ar_gather(1)
 
         chains = [(block(i * BU + u, NODES), i * BU + u, p) for u in range(BU) for p in range(PAIRS)]
-        outs, dps = [], []
+        dps = []
         for r, s, p in chains:
             ls = lanes[p]
             oh, ol = split(datt[r, ls])
             oh, ol = apart(oh), apart(ol)
-            outs.append((oh, ol))
             high = vh[r, ls]
             dps.append(nt(lanes_cat(high, vl[r, ls], high), lanes_cat(oh, oh, ol)))
         dss = []
         for (r, s, p), dp in zip(chains, dps):
             pr = prob[s, p, 0].astype(F32) + prob[s, p, 1].astype(F32)
             dss.append(split(pr * (dp - jnp.sum(pr * dp, axis=0, keepdims=True))))
-        for (r, s, p), (oh, ol) in zip(chains, outs):
-            got = nn(prob[s, p, 0], lanes_cat(oh, ol))
-            dv[r, lanes[p]] = got[:, 0:128] + got[:, 128:256] + nn(prob[s, p, 1], oh)
         for (r, s, p), (high, low) in zip(chains, dss):
             ls = lanes[p]
             qbh = apart(qh[r, ls])
@@ -748,9 +758,9 @@
         mixo[r, :] = (x[r, :].astype(F32) + got).astype(BF)
         return 0
 
+    w_middle(VALUE)
     lax.fori_loop(0, NR, out_block, 0)
     store(mixo, layer_out)
-    w_middle(VALUE)
     w_gather(GATE)
     w_gather(OUT)
     w_spread(KEY)
@@ -904,6 +914,7 @@
             VM((R, W), F32),
             VM((R, W), F32),
             VM((NB, PAIRS, 2, NODES, 2 * NODES), BF),
+            VM((R, W), F32),
             VM((R, W), F32),
             VM((4, R, W), BF),
             VM((R, W), BF),

time: 70.7 us -> 70.2 us (level)
  no operation moved by 1% of the time
where the time goes in v6:
time: 70.2 us; the launch traced here: 70 us
  Pallas kernels  69.4 us (99%)
    pallas_call x1, Pallas kernels, shards(): pl.pallas_call(functools.partial(layer_kernel, groups), name='layer_kerne...  66.1 us
    pallas_call x1, Pallas kernels, shards(): pl.pallas_call(finish_kernel, name='finish_kernel', out_shape=(jax.ShapeD...  3.33 us

profile of v6, /device:TPU:0, one launch (start us, length us, event | category | flops | bytes accessed | tf_op | source)
XLA Modules:
  0.0 70.0 jit_solution(14948348700660752792)
XLA Ops:
  0.6 66.1 %layer_kernel.1 = (bf16[2048,256]{1,0:T(8,128)(2,1)}, bf16[2048,256]{1,0:T(8,128)(2,1)}, f32[256]{0:T(256)}, f32[256]{0:T(256)}, bf16[5,512,256]{2,1,0:T(8,128)(2,1)}) custom-call(bf16[2048,256]{1,0:T(8,128)(2,1)} %x_hbm.1, bf16[2048,256]{1,0:T(8,128)(2,1)} %c_hbm.1, bf16[256]{0:T(256)(128)(2,1)} %gain_hbm.1, bf16[256]{0:T(256)(128)(2,1)} %bias_hbm.1, ...), custom_call_target="tpu_custom_call" | custom-call | tf_op jit(solution)/shard_map/layer_kernel/pallas_call | solution.py:870
  66.7 3.3 %finish_kernel.1 = (bf16[2048,256]{1,0:T(8,128)(2,1)}, bf16[2048,256]{1,0:T(8,128)(2,1)}, f32[256]{0:T(256)}, f32[256]{0:T(256)}, f32[512,256]{1,0:T(8,128)}, /*...) custom-call(bf16[2048,256]{1,0:T(8,128)(2,1)} %get-tuple-element.14.lo_in, ...), custom_call_target="tpu_custom_call" | custom-call | tf_op jit(solution)/shard_map/finish_kernel/pallas_call | solution.py:969

commit v7 on v6

--- a/solution.py
+++ b/solution.py
@@ -532,32 +532,19 @@
     ar_scatter(1)
     send(mix, mixo, mix_sems.at[0], mix_sems.at[1], partner)
 
-    KB = 1024
-
-    def weight_grads(kinds):
-        def step(i, _):
-            r = block(i, KB)
-            n = normed[r, :]
-            for kind in kinds:
-                got = tn(n, low4[kind, r, :])
-                part[kind, own_rows, :] += got[0:W]
-                part[kind, oth_rows, :] += got[W : 2 * W]
-            return 0
-
-        for kind in kinds:
-            part[kind] = jnp.zeros(part.shape[1:], F32)
-        lax.fori_loop(0, R // KB, step, 0)
+
+    def keep_part(kind, rows, got):
+        part[kind, rows, :] = got
+        psend[kind, rows, :] = got.astype(BF)
+
+    def weight_grads(kind):
+        got = tn(normed[...], low4[kind])
+        keep_part(kind, own_rows, got[0:W])
+        keep_part(kind, oth_rows, got[W : 2 * W])
 
     def out_grads():
-        def step(i, _):
-            r = block(i, KB)
-            cc = c[r, :]
-            part[OUT, own_rows, :] += tn(mix[r, :], cc)
-            part[OUT, oth_rows, :] += tn(mixo[r, :], cc)
-            return 0
-
-        part[OUT] = jnp.zeros(part.shape[1:], F32)
-        lax.fori_loop(0, R // KB, step, 0)
+        keep_part(OUT, own_rows, tn(mix[...], c[...]))
+        keep_part(OUT, oth_rows, tn(mixo[...], c[...]))
 
     D = 2 * W
     PA = D // A
@@ -570,7 +557,6 @@
         return (second, first) if w in B_FIRST else (first, second)
 
     def w_scatter(w):
-        psend[w] = part[w].astype(BF)
         for i, (j, to) in enumerate(order(w)[0][1]):
             send(
                 psend.at[w, block(j, PA)],
@@ -645,7 +631,7 @@
         wait_both(fin.at[w, pl.ds(0, (A - 1) * PA)], w_sems, (w, 3))
         store(fin.at[w], fin_hbm.at[w])
 
-    weight_grads((GATE,))
+    weight_grads(GATE)
     w_scatter(GATE)
     bytes_of(mixo, mix_sems.at[1])
     out_grads()
@@ -694,7 +680,7 @@
 
     lax.fori_loop(0, NB // BU, backward_block, 0)
     w_middle(OUT)
-    weight_grads((QUERY,))
+    weight_grads(QUERY)
     w_scatter(QUERY)
     w_spread(GATE)
 
@@ -715,9 +701,9 @@
         return 0
 
     lax.fori_loop(0, NB // KU, key_block, 0)
-    weight_grads((KEY,))
+    weight_grads(KEY)
     w_scatter(KEY)
-    weight_grads((VALUE,))
+    weight_grads(VALUE)
     w_scatter(VALUE)
     w_spread(OUT)
 
@@ -795,6 +781,7 @@
     store(co, input_grad)
     w_spread(VALUE)
     w_gather(KEY)
+    w_gather(QUERY)
 
     row = lax.broadcasted_iota(jnp.int32, (8, W), 0)
     total = jnp.where(row == 0, carry[0], jnp.where(row == 1, carry[1], 0.0))
@@ -815,7 +802,6 @@
 
     in_order(total, 0, gb_recv, al, A, a_peers)
     w_gather(VALUE)
-    w_gather(QUERY)
     in_order(added(0, gb_recv, A), 1, gb_z, bl, B, b_peers)
     w_keep(GATE)
     w_keep(OUT)

time: 70.2 us -> 70.7 us (level)
  no operation moved by 1% of the time
where the time goes in v7:
time: 70.7 us; the launch traced here: 70.5 us
  Pallas kernels  69.7 us (99%)
  between operations  0.82 us (1%)
    pallas_call x1, Pallas kernels, shards(): pl.pallas_call(functools.partial(layer_kernel, groups), name='layer_kerne...  66.4 us
    pallas_call x1, Pallas kernels, shards(): pl.pallas_call(finish_kernel, name='finish_kernel', out_shape=(jax.ShapeD...  3.33 us

profile of v7, /device:TPU:0, one launch (start us, length us, event | category | flops | bytes accessed | tf_op | source)
XLA Modules:
  0.0 70.5 jit_solution(7768624860436172436)
XLA Ops:
  0.6 66.4 %layer_kernel.1 = (bf16[2048,256]{1,0:T(8,128)(2,1)}, bf16[2048,256]{1,0:T(8,128)(2,1)}, f32[256]{0:T(256)}, f32[256]{0:T(256)}, bf16[5,512,256]{2,1,0:T(8,128)(2,1)}) custom-call(bf16[2048,256]{1,0:T(8,128)(2,1)} %x_hbm.1, bf16[2048,256]{1,0:T(8,128)(2,1)} %c_hbm.1, bf16[256]{0:T(256)(128)(2,1)} %gain_hbm.1, bf16[256]{0:T(256)(128)(2,1)} %bias_hbm.1, ...), custom_call_target="tpu_custom_call" | custom-call | tf_op jit(solution)/shard_map/layer_kernel/pallas_call | solution.py:856
  67.1 3.3 %finish_kernel.1 = (bf16[2048,256]{1,0:T(8,128)(2,1)}, bf16[2048,256]{1,0:T(8,128)(2,1)}, f32[256]{0:T(256)}, f32[256]{0:T(256)}, f32[512,256]{1,0:T(8,128)}, /*...) custom-call(bf16[2048,256]{1,0:T(8,128)(2,1)} %get-tuple-element.14.lo_in, ...), custom_call_target="tpu_custom_call" | custom-call | tf_op jit(solution)/shard_map/finish_kernel/pallas_call | solution.py:955
